TPU v7x, 512 devices: a whole 4x8x8 slice. The times are simulated.
512 devices in a mesh: rep: 32 (over y_lo, z, core), fsdp: 16 (over y_hi, x).
Axes of the slice: x: 4, y: 8 (y_hi: 4, y_lo: 2; y = y_hi * 2 + y_lo), z: 8, core: 2. Of those that a mesh axis runs over, the one named last changes fastest.
Arguments:
- tokens: bfloat16 [98304, 2048], P(('rep', 'fsdp')), may hold values from -6 to 6
- weight: bfloat16 [65536, 2048], P(('rep', 'fsdp')), may hold values from -6 to 6
- gain: bfloat16 [65536], P(('rep', 'fsdp')), may hold values from 0.5 to 1.5
- upstream: bfloat16 [98304, 2048], P(('rep', 'fsdp')), may hold values from -6 to 6
- step: int32 [1], replicated, may hold values from 0 to 63
Outputs:
- projected: bfloat16 [98304, 2048], P(('rep', 'fsdp'))
- input_gradient: bfloat16 [98304, 2048], P(('rep', 'fsdp'))
- new_weight: bfloat16 [65536, 2048], P(('rep', 'fsdp'))
- new_gain: bfloat16 [65536], P(('rep', 'fsdp'))
All inputs are finite; a program needn't handle non-finite values.
Results may differ from a plain program's by a relative error of at most 0.0058.
Values may be sent and summed in bfloat16 or wider, within the bound.
No kernel may reach another device: no remote copies, remote signals or barrier semaphores. Data moves between devices by JAX's collectives and lax.ppermute only.
A program may use at most 128 MiB of HBM per device.

v0:
```python
import math

import jax
import jax.numpy as jnp
from jax import lax
from jax.sharding import PartitionSpec as P

eps = 1e-05
step_rate = 0.75
gain_rate = 0.004


def for_sending(value):
    return jax.tree.map(lambda a: a.astype(jnp.bfloat16) if a.dtype == jnp.float32 else a, value)


def shifted(value, axis, steps):
    count = lax.axis_size(axis)
    pairs = [(source, (source + steps) % count) for source in range(count)]
    return lax.ppermute(value, axis, pairs)


def gossip_branch(distance):

    def branch(params):
        return jax.tree.map(
            lambda part, own: part.astype(own.dtype),
            shifted(for_sending(params), "rep", distance),
            params,
        )

    return branch


def weight_partial(normed_rows, upstream, scale):
    return (
        lax.dot_general(
            normed_rows, upstream, (((0,), (0,)), ((), ())), preferred_element_type=jnp.float32
        )
        * scale
    ).astype(jnp.bfloat16)


def on_device(tokens, weight, gain, upstream, step):
    members = lax.axis_size("fsdp")
    shard_rows = weight.shape[0]
    width_in = shard_rows * members
    width_out = weight.shape[1]
    scale = 1.0 / math.sqrt(width_in)
    input_float = tokens.astype(jnp.float32)
    inverse_deviation = lax.rsqrt(jnp.mean(input_float * input_float, axis=1, keepdims=True) + eps)
    normalized_input = input_float * inverse_deviation
    full_weight, full_gain = (
        lax.all_gather(weight, "fsdp", axis=0, tiled=True),
        lax.all_gather(gain, "fsdp", axis=0, tiled=True),
    )
    gain_float = full_gain.astype(jnp.float32)
    normed_rows = (normalized_input * gain_float).astype(jnp.bfloat16)
    summed = jnp.dot(normed_rows, full_weight, preferred_element_type=jnp.float32)
    normed_gradient = (
        lax.dot_general(
            upstream, full_weight, (((1,), (1,)), ((), ())), preferred_element_type=jnp.float32
        )
        * scale
    )
    projected = (summed * scale).astype(jnp.bfloat16)
    scaled_rows = gain_float * normed_gradient
    input_gradient = (
        inverse_deviation
        * (
            scaled_rows
            - normalized_input * jnp.mean(scaled_rows * normalized_input, axis=1, keepdims=True)
        )
    ).astype(jnp.bfloat16)
    gain_portion = jnp.sum(normed_gradient * normalized_input, axis=0).astype(jnp.bfloat16)
    part_w = weight_partial(normed_rows, upstream, scale)
    pieces_w, pieces_g = (
        lax.all_to_all(
            part_w.reshape(members, shard_rows, width_out),
            "fsdp",
            split_axis=0,
            concat_axis=0,
            tiled=True,
        ),
        lax.all_to_all(
            gain_portion.reshape(members, shard_rows),
            "fsdp",
            split_axis=0,
            concat_axis=0,
            tiled=True,
        ),
    )
    grad_w = jnp.sum(pieces_w.astype(jnp.float32), axis=0)
    grad_g = jnp.sum(pieces_g.astype(jnp.float32), axis=0)
    stepped_w = (weight.astype(jnp.float32) - step_rate * grad_w).astype(jnp.bfloat16)
    stepped_g = (gain.astype(jnp.float32) - gain_rate * grad_g).astype(jnp.bfloat16)
    branches = [gossip_branch(distance) for distance in (1, 2, 4, 8)]
    peer_w, peer_g = lax.switch(step[0] % 4, branches, (stepped_w, stepped_g))
    new_weight = (0.5 * (stepped_w.astype(jnp.float32) + peer_w.astype(jnp.float32))).astype(
        jnp.bfloat16
    )
    new_gain = (0.5 * (stepped_g.astype(jnp.float32) + peer_g.astype(jnp.float32))).astype(
        jnp.bfloat16
    )
    return (projected, input_gradient, new_weight, new_gain)


def solution(mesh):
    placed = (
        P(("rep", "fsdp"), None),
        P(("rep", "fsdp"), None),
        P(("rep", "fsdp")),
        P(("rep", "fsdp"), None),
        P(),
    )
    return jax.shard_map(
        on_device,
        mesh=mesh,
        in_specs=placed,
        out_specs=(
            P(("rep", "fsdp"), None),
            P(("rep", "fsdp"), None),
            P(("rep", "fsdp"), None),
            P(("rep", "fsdp")),
        ),
        check_vma=False,
    )
```

profile of v0, /device:TPU:8, one launch (start us, length us, event | category | flops | bytes accessed | tf_op | source)
XLA Modules:
  0.0 372.8 jit_solution(9312939321411646770)
XLA Ops:
  7.2 0.0 copy-start
  7.2 0.0 all-gather.3.cloned.1.call-start
  7.2 0.7 all-gather.3.cloned.1.call-update
  7.9 44.0 %all-gather = bf16[16,1,128]{2,1,0:T(2,128)(2,1)S(1)} all-gather(bf16[1,1,128]{2,1,0:T(2,128)(2,1)} %bitcast.19), channel_id=1, replica_groups=mesh['rep'=32,'fsdp'=16] {'fsdp'}, dimensions={0}, use_global_device_ids=true | all-gather | bytes 4352 | tf_op jit(solution)/shard_map/all_gather | solution.py:55
  51.9 1.4 fusion.11
  53.3 6.9 %multiply_convert_fusion = bf16[2048,2048]{1,0:T(8,128)(2,1)} fusion(bf16[192,2048]{1,0:T(8,128)(2,1)S(1)} %copy-done, bf16[192,2048]{1,0:T(8,128)(2,1)} %param.9, f32[2048]{0:T(1024)S(1)} %bitcast.15, f32[192]{0:T(256)S(1)} %add_rsqrt_fusion), kind=kOutput, calls=%fused_computation.1 | convolution fusion | flops 1620574208 | bytes 9970432 | tf_op jit(solution)/shard_map/dot_general | solution.py:37
  60.2 4.9 %all-to-all-start = ((bf16[16,128,2048]{2,1,0:T(8,128)(2,1)}), bf16[16,128,2048]{2,1,0:T(8,128)(2,1)}, u32[]{:S(2)}, u32[]{:S(2)}) async-start(bf16[16,128,2048]{2,1,0:T(8,128)(2,1)} %bitcast.14), calls=%async_computation | async-start | bytes 16777216 | tf_op jit(solution)/shard_map/all_to_all | solution.py:78
  65.8 147.8 %all-gather.3.cloned.1.call-done = bf16[2048,2048]{1,0:T(8,128)(2,1)} async-done(((bf16[128,2048]{1,0:T(8,128)(2,1)}), bf16[2048,2048]{1,0:T(8,128)(2,1)}) %all-gather.3.cloned.1.call-update) | async-done | bytes 8388624 | tf_op jit(solution)/shard_map/all_gather | solution.py:54
  213.6 6.7 %fusion.10 = (bf16[2048]{0:T(1024)(128)(2,1)S(1)}, f32[192]{0:T(256)S(1)}, f32[192,2048]{1,0:T(8,128)S(1)}) fusion(bf16[192,2048]{1,0:T(8,128)(2,1)S(1)} %copy-done.1, f32[192]{0:T(256)S(1)} %add_rsqrt_fusion, f32[2048]{0:T(1024)S(1)} %broadcast_multiply_fusion, bf16[192,2048]{1,0:T(8,128)(2,1)S(1)} %copy-done, ...), kind=kOutput, calls=%fused_computation.15 | convolution fusion | flops 1613756160 | bytes 11548160 | tf_op jit(solution)/shard_map/dot_general | solution.py:61
  220.3 0.6 copy.9
  220.9 1.3 fusion.9
  222.2 2.8 fusion
  225.0 36.9 %all-to-all-done = bf16[16,128,2048]{2,1,0:T(8,128)(2,1)} async-done(((bf16[16,128,2048]{2,1,0:T(8,128)(2,1)}), bf16[16,128,2048]{2,1,0:T(8,128)(2,1)}, u32[]{:S(2)}, u32[]{:S(2)}) %all-to-all-start) | async-done | bytes 8388640 | tf_op jit(solution)/shard_map/all_to_all | solution.py:78
  261.9 47.8 %all-to-all-start.1 = ((bf16[16,1,128]{2,1,0:T(2,128)(2,1)}), bf16[16,1,128]{2,1,0:T(2,128)(2,1)S(1)}, u32[]{:S(2)}, u32[]{:S(2)}) async-start(bf16[16,1,128]{2,1,0:T(2,128)(2,1)} %copy.9), calls=%async_computation.1 | async-start | bytes 16384 | tf_op jit(solution)/shard_map/all_to_all | solution.py:85
  309.7 0.0 copy-start.2
  309.7 5.4 %convert_reduce_fusion = f32[128,2048]{1,0:T(8,128)S(1)} fusion(bf16[16,128,2048]{2,1,0:T(8,128)(2,1)} %all-to-all-done), kind=kLoop, calls=%fused_computation | loop fusion | flops 8126464 | bytes 9437184 | tf_op jit(solution)/shard_map/reduce_sum | solution.py:93
  315.1 0.1 subtract_convert_fusion
  315.3 6.0 %all-to-all-done.1 = bf16[16,1,128]{2,1,0:T(2,128)(2,1)S(1)} async-done(((bf16[16,1,128]{2,1,0:T(2,128)(2,1)}), bf16[16,1,128]{2,1,0:T(2,128)(2,1)S(1)}, u32[]{:S(2)}, u32[]{:S(2)}) %all-to-all-start.1) | async-done | bytes 4128 | tf_op jit(solution)/shard_map/all_to_all | solution.py:85
  321.4 41.5 %conditional.4 = (bf16[128,2048]{1,0:T(8,128)(2,1)}, bf16[128]{0:T(256)(128)(2,1)}) conditional(s32[]{:T(128)} %clamp.3, (bf16[128,2048]{1,0:T(8,128)(2,1)S(1)}, bf16[128]{0:T(256)(128)(2,1)S(1)}) %tuple.50, (bf16[128,2048]{1,0:T(8,128)(2,1)S(1)}, bf16[128]{0:T(256)(128)(2,1)S(1)}) %tuple.50, ...), branch_computations={%region_5.6_spmd, %region_6.7_spmd, %region_7.8_spmd, %region_8.9_... | conditional | bytes 2098272
  321.4 20.9 %collective-permute-start.4 = (bf16[128,2048]{1,0:T(8,128)(2,1)S(1)}, bf16[128,2048]{1,0:T(8,128)(2,1)}, u32[]{:S(2)}, u32[]{:S(2)}) collective-permute-start(bf16[128,2048]{1,0:T(8,128)(2,1)S(1)} %get-tuple-element.32), channel_id=1, source_target_pairs={{0,64},{16,80},{32,96},{48,112},{64,128},{80,144},{96,160},{112,17... | collective-permute-start | bytes 1572872 | tf_op jit(solution)/shard_map/cond/branch_2_fun/ppermute | solution.py:20
  342.3 1.9 collective-permute-start.5
  344.2 18.6 %collective-permute-done.5 = bf16[128]{0:T(256)(128)(2,1)} collective-permute-done((bf16[128]{0:T(256)(128)(2,1)S(1)}, bf16[128]{0:T(256)(128)(2,1)}, u32[]{:S(2)}, u32[]{:S(2)}) %collective-permute-start.5) | collective-permute-done | bytes 288 | tf_op jit(solution)/shard_map/cond/branch_2_fun/ppermute | solution.py:20
  362.8 1.2 fusion.17
  364.0 2.0 fusion.13
  (15 shorter events, 0.1 us)
Async XLA Ops:
  7.2 46.2 %copy-start = (bf16[192,2048]{1,0:T(8,128)(2,1)S(1)}, bf16[192,2048]{1,0:T(8,128)(2,1)}, u32[]{:S(2)}) copy-start(bf16[192,2048]{1,0:T(8,128)(2,1)} %param.12) | copy-start | bytes 2359300
  7.2 206.4 %all-gather.3.cloned.1.call-start = ((), (), s32[]{:S(2)}) async-start(), calls=%async_computation.2 | async-start | bytes 8912896 | tf_op jit(solution)/shard_map/all_gather | solution.py:54
  60.2 153.4 %copy-start.1 = (bf16[192,2048]{1,0:T(8,128)(2,1)S(1)}, bf16[192,2048]{1,0:T(8,128)(2,1)}, u32[]{:S(2)}) copy-start(bf16[192,2048]{1,0:T(8,128)(2,1)} %param.9) | copy-start | bytes 2359300
  60.2 201.8 %all-to-all-start = ((bf16[16,128,2048]{2,1,0:T(8,128)(2,1)}), bf16[16,128,2048]{2,1,0:T(8,128)(2,1)}, u32[]{:S(2)}, u32[]{:S(2)}) async-start(bf16[16,128,2048]{2,1,0:T(8,128)(2,1)} %bitcast.14), calls=%async_computation | async-start | bytes 16777216 | tf_op jit(solution)/shard_map/all_to_all | solution.py:78
  213.6 8.6 %copy-start.4 = (bf16[2048,2048]{1,0:T(8,128)(2,1)S(1)}, bf16[2048,2048]{1,0:T(8,128)(2,1)}, u32[]{:S(2)}) copy-start(bf16[2048,2048]{1,0:T(8,128)(2,1)} %all-gather.3.cloned.1.call-done) | copy-start | bytes 25165828
  261.9 59.4 %all-to-all-start.1 = ((bf16[16,1,128]{2,1,0:T(2,128)(2,1)}), bf16[16,1,128]{2,1,0:T(2,128)(2,1)S(1)}, u32[]{:S(2)}, u32[]{:S(2)}) async-start(bf16[16,1,128]{2,1,0:T(2,128)(2,1)} %copy.9), calls=%async_computation.1 | async-start | bytes 16384 | tf_op jit(solution)/shard_map/all_to_all | solution.py:85
  309.7 5.4 %copy-start.2 = (bf16[128,2048]{1,0:T(8,128)(2,1)S(1)}, bf16[128,2048]{1,0:T(8,128)(2,1)}, u32[]{:S(2)}) copy-start(bf16[128,2048]{1,0:T(8,128)(2,1)} %param.10) | copy-start | bytes 1572868
  315.1 6.2 %copy-start.3 = (bf16[128]{0:T(256)(128)(2,1)S(1)}, bf16[128]{0:T(256)(128)(2,1)}, u32[]{:S(2)}) copy-start(bf16[128]{0:T(256)(128)(2,1)} %param.11) | copy-start | bytes 772
  321.4 41.4 %collective-permute-start.4 = (bf16[128,2048]{1,0:T(8,128)(2,1)S(1)}, bf16[128,2048]{1,0:T(8,128)(2,1)}, u32[]{:S(2)}, u32[]{:S(2)}) collective-permute-start(bf16[128,2048]{1,0:T(8,128)(2,1)S(1)} %get-tuple-element.32), channel_id=1, source_target_pairs={{0,64},{16,80},{32,96},{48,112},{64,128},{80,144},{96,160},{112,17... | collective-permute-start | bytes 1572872 | tf_op jit(solution)/shard_map/cond/branch_2_fun/ppermute | solution.py:20
  342.3 20.6 %collective-permute-start.5 = (bf16[128]{0:T(256)(128)(2,1)S(1)}, bf16[128]{0:T(256)(128)(2,1)}, u32[]{:S(2)}, u32[]{:S(2)}) collective-permute-start(bf16[128]{0:T(256)(128)(2,1)S(1)} %get-tuple-element.33), channel_id=1, source_target_pairs={{0,64},{16,80},{32,96},{48,112},{64,128},{80,144},{96,160},{112,17... | collective-permute-start | bytes 776 | tf_op jit(solution)/shard_map/cond/branch_2_fun/ppermute | solution.py:20
Sparse Core Ops, SparseCore 0:
  11.0 202.4 all-gather.2
where the time goes:
time: 373 us
  waiting for transfers between devices  210 us (56%)
  starting transfers between devices  75.5 us (20%)
  blocking collectives  44 us (12%)
  matrix products  16.4 us (4%)
  between operations  14.8 us (4%)
  other arithmetic  11.4 us (3%)
    all_gather x1, waiting for transfers between devices, on_device(): lax.all_gather(weight, 'fsdp', axis=0, tiled=True)  148 us
    all_to_all x1, starting transfers between devices, on_device(): lax.all_to_all(gain_portion.reshape(members, shard_rows), 'fsdp', split_a...  47.8 us
    all_gather x1, blocking collectives, on_device(): lax.all_gather(gain, 'fsdp', axis=0, tiled=True)  44 us
    all_to_all x1, waiting for transfers between devices, on_device(): lax.all_to_all(part_w.reshape(members, shard_rows, width_out), 'fsdp', sp...  36.9 us
    ppermute x2, starting transfers between devices, shifted(): return lax.ppermute(value, axis, pairs)  22.8 us
    ppermute x2, waiting for transfers between devices, shifted(): return lax.ppermute(value, axis, pairs)  18.6 us
  transfers between devices with their start and end apart: 5, of which 4 were waited for; matrix products, arithmetic and copies ran while one was open for 7% of the time, Pallas kernels for 0%

commit v1 on v0

v1 whole, which is shorter than its diff:
```python
import math

import jax
import jax.numpy as jnp
from jax import lax
from jax.sharding import Mesh
from jax.sharding import PartitionSpec as P

eps = 1e-05
step_rate = 0.75
gain_rate = 0.004
F32 = jnp.float32
BF16 = jnp.bfloat16


def shifted(value, axis, steps):
    count = lax.axis_size(axis)
    pairs = [(source, (source + steps) % count) for source in range(count)]
    return lax.ppermute(value, axis, pairs)


def gossip_branch(distance):
    def branch(params):
        return jax.tree.map(lambda part: shifted(part, "rep", distance), params)

    return branch


def exchange(blocks, axis):
    return lax.all_to_all(blocks, axis, split_axis=0, concat_axis=0, tiled=True)


def on_device(tokens, weight, gain, upstream, step):
    n_x, n_y = lax.axis_size("x"), lax.axis_size("yh")
    rows, width_out = weight.shape
    count, width_in = tokens.shape
    scale = 1.0 / math.sqrt(width_in)
    me = lax.axis_index("x")

    offsets = (1, n_x - 1, 2)
    arrived = [shifted(upstream, "x", d) for d in offsets]
    full_weight = lax.all_gather(weight, "yh", axis=0, tiled=True)
    full_gain = lax.all_gather(gain, "yh", axis=0, tiled=True).astype(F32)

    input_float = tokens.astype(F32)
    inverse_deviation = lax.rsqrt(jnp.mean(input_float * input_float, axis=1, keepdims=True) + eps)
    normalized_input = input_float * inverse_deviation
    sent = normalized_input.astype(BF16).reshape(count, n_y, n_x, rows)
    sent = sent.transpose(2, 0, 1, 3).reshape(n_x, count, n_y * rows)
    xhat = exchange(sent, "x").reshape(n_x * count, n_y * rows).astype(F32)
    normed_rows = (xhat * full_gain).astype(BF16)

    gathered = jnp.zeros((n_x, count, width_out), BF16)
    gathered = lax.dynamic_update_slice(gathered, upstream[None], (me, 0, 0))
    for d, block in zip(offsets, arrived):
        gathered = lax.dynamic_update_slice(gathered, block[None], ((me + n_x - d) % n_x, 0, 0))
    gathered = gathered.reshape(n_x * count, width_out)

    part_w = (
        lax.dot_general(normed_rows, gathered, (((0,), (0,)), ((), ())), preferred_element_type=F32)
        * scale
    ).astype(BF16)
    grad_w = lax.psum_scatter(part_w, "yh", scatter_dimension=0, tiled=True).astype(F32)
    stepped_w = (weight.astype(F32) - step_rate * grad_w).astype(BF16)

    part_p = (jnp.dot(normed_rows, full_weight, preferred_element_type=F32) * scale).astype(BF16)
    normed_gradient = (
        lax.dot_general(gathered, full_weight, (((1,), (1,)), ((), ())), preferred_element_type=F32)
        * scale
    )
    part_g = jnp.sum(normed_gradient * xhat, axis=0).astype(BF16)
    scaled = (full_gain * normed_gradient).astype(BF16).reshape(n_x, count, n_y * rows)
    scaled_back = exchange(scaled, "x")
    pieces_p = exchange(part_p.reshape(n_x, count, width_out), "x")
    pieces_g = exchange(part_g.reshape(n_y, rows), "yh")

    projected = jnp.sum(pieces_p.astype(F32), axis=0).astype(BF16)
    scaled_rows = scaled_back.reshape(n_x, count, n_y, rows).transpose(1, 2, 0, 3)
    scaled_rows = scaled_rows.reshape(count, width_in).astype(F32)
    input_gradient = (
        inverse_deviation
        * (
            scaled_rows
            - normalized_input * jnp.mean(scaled_rows * normalized_input, axis=1, keepdims=True)
        )
    ).astype(BF16)
    grad_g = jnp.sum(pieces_g.astype(F32), axis=0)
    stepped_g = (gain.astype(F32) - gain_rate * grad_g).astype(BF16)

    branches = [gossip_branch(distance) for distance in (1, 2, 4, 8)]
    peer_w, peer_g = lax.switch(step[0] % 4, branches, (stepped_w, stepped_g))
    new_weight = (0.5 * (stepped_w.astype(F32) + peer_w.astype(F32))).astype(BF16)
    new_gain = (0.5 * (stepped_g.astype(F32) + peer_g.astype(F32))).astype(BF16)
    return (projected, input_gradient, new_weight, new_gain)


def solution(mesh):
    n_rep, n_fsdp = mesh.devices.shape
    n_x = 4
    split = Mesh(mesh.devices.reshape(n_rep, n_fsdp // n_x, n_x), ("rep", "yh", "x"))
    every = ("rep", "yh", "x")
    placed = (P(every, None), P(every, None), P(every), P(every, None), P())
    return jax.shard_map(
        on_device,
        mesh=split,
        in_specs=placed,
        out_specs=(P(every, None), P(every, None), P(every, None), P(every)),
        check_vma=False,
    )
```

time: 373 us -> 174 us (0.47)
  the two profiles are of different devices: /device:TPU:8 before, /device:TPU:60 now
where the time goes in v1:
time: 174 us; the launch traced here: 173 us
  waiting for transfers between devices  61.2 us (35%)
  starting transfers between devices  38.5 us (22%)
  blocking collectives  20.1 us (12%)
  between operations  14.9 us (9%)
  matrix products  14.5 us (8%)
  other arithmetic  12.2 us (7%)
  local copies, waits for them, and re-layouts  12 us (7%)
    ppermute x5, waiting for transfers between devices, shifted(): return lax.ppermute(value, axis, pairs)  26.3 us
    ppermute x5, starting transfers between devices, shifted(): return lax.ppermute(value, axis, pairs)  20.1 us
    all_to_all x3, starting transfers between devices, exchange(): return lax.all_to_all(blocks, axis, split_axis=0, concat_axis=0, tiled=True)  18.4 us
    all_gather x1, waiting for transfers between devices, on_device(): full_weight = lax.all_gather(weight, 'yh', axis=0, tiled=True)  15.1 us
    reduce_scatter x1, waiting for transfers between devices, on_device(): lax.psum_scatter(part_w, 'yh', scatter_dimension=0, tiled=True).astype(F32)  13.5 us
    all_to_all x1, blocking collectives, exchange(): return lax.all_to_all(blocks, axis, split_axis=0, concat_axis=0, tiled=True)  10.2 us
    all_gather x1, blocking collectives, on_device(): full_gain = lax.all_gather(gain, 'yh', axis=0, tiled=True).astype(F32)  9.93 us
    all_to_all x3, waiting for transfers between devices, exchange(): return lax.all_to_all(blocks, axis, split_axis=0, concat_axis=0, tiled=True)  6.33 us
  transfers between devices with their start and end apart: 10, of which 6 were waited for; matrix products, arithmetic and copies ran while one was open for 20% of the time, Pallas kernels for 0%

profile of v1, /device:TPU:60, one launch (start us, length us, event | category | flops | bytes accessed | tf_op | source)
XLA Modules:
  0.0 173.3 jit_solution(12991521172907473789)
XLA Ops:
  7.2 3.1 %collective-permute-start.8 = (bf16[192,2048]{1,0:T(8,128)(2,1)}, bf16[192,2048]{1,0:T(8,128)(2,1)}, u32[]{:S(2)}, u32[]{:S(2)}) collective-permute-start(bf16[192,2048]{1,0:T(8,128)(2,1)} %param.12), channel_id=1, source_target_pairs={{0,1},{1,2},{2,3},{3,0},{4,5},{5,6},{6,7},{7,4},{8,9},{9,10},{10,1... | collective-permute-start | bytes 2359304 | tf_op jit(solution)/shard_map/ppermute | solution.py:19
  10.3 2.7 %collective-permute-start.9 = (bf16[192,2048]{1,0:T(8,128)(2,1)}, bf16[192,2048]{1,0:T(8,128)(2,1)}, u32[]{:S(2)}, u32[]{:S(2)}) collective-permute-start(bf16[192,2048]{1,0:T(8,128)(2,1)} %param.12), channel_id=1, source_target_pairs={{0,3},{1,0},{2,1},{3,2},{4,7},{5,4},{6,5},{7,6},{8,11},{9,8},{10,9... | collective-permute-start | bytes 2359304 | tf_op jit(solution)/shard_map/ppermute | solution.py:19
  13.1 3.6 %collective-permute-start.10 = (bf16[192,2048]{1,0:T(8,128)(2,1)}, bf16[192,2048]{1,0:T(8,128)(2,1)}, u32[]{:S(2)}, u32[]{:S(2)}) collective-permute-start(bf16[192,2048]{1,0:T(8,128)(2,1)} %param.12), channel_id=1, source_target_pairs={{0,2},{1,3},{2,0},{3,1},{4,6},{5,7},{6,4},{7,5},{8,10},{9,11},{10,... | collective-permute-start | bytes 2359304 | tf_op jit(solution)/shard_map/ppermute | solution.py:19
  21.5 6.0 %all-to-all-start = ((bf16[4,192,512]{2,1,0:T(8,128)(2,1)}), bf16[4,192,512]{2,1,0:T(8,128)(2,1)}, u32[]{:S(2)}, u32[]{:S(2)}) async-start(bf16[4,192,512]{2,1,0:T(8,128)(2,1)} %reshape.67), calls=%async_computation | async-start | bytes 1572864 | tf_op jit(solution)/shard_map/all_to_all | solution.py:30
  27.5 9.9 %all-gather = bf16[4,1,128]{2,1,0:T(2,128)(2,1)S(1)} all-gather(bf16[1,1,128]{2,1,0:T(2,128)(2,1)S(1)} %bitcast.48), channel_id=1, replica_groups=mesh['rep'=32,'yh'=4,'x'=4] {'yh'}, dimensions={0}, use_global_device_ids=true | all-gather | bytes 1280 | tf_op jit(solution)/shard_map/all_gather | solution.py:43
  39.0 7.2 %collective-permute-done.8 = bf16[192,2048]{1,0:T(8,128)(2,1)} collective-permute-done((bf16[192,2048]{1,0:T(8,128)(2,1)}, bf16[192,2048]{1,0:T(8,128)(2,1)}, u32[]{:S(2)}, u32[]{:S(2)}) %collective-permute-start.8) | collective-permute-done | bytes 786464 | tf_op jit(solution)/shard_map/ppermute | solution.py:19
  49.9 4.2 %all-to-all-done = bf16[4,192,512]{2,1,0:T(8,128)(2,1)} async-done(((bf16[4,192,512]{2,1,0:T(8,128)(2,1)}), bf16[4,192,512]{2,1,0:T(8,128)(2,1)}, u32[]{:S(2)}, u32[]{:S(2)}) %all-to-all-start) | async-done | bytes 786464 | tf_op jit(solution)/shard_map/all_to_all | solution.py:30
  54.1 4.3 %fusion = bf16[512,2048]{1,0:T(8,128)(2,1)} fusion(bf16[4,192,2048]{2,1,0:T(8,128)(2,1)S(1)} %bitcast_dynamic-update-slice_fusion, bf16[4,192,512]{2,1,0:T(8,128)(2,1)} %all-to-all-done, f32[512]{0:T(512)S(1)} %bitcast.44), kind=kOutput, calls=%fused_computation.2 | convolution fusion | flops 1613889536 | bytes 6031360 | tf_op jit(solution)/shard_map/dot_general | solution.py:60
  58.5 15.1 %all-gather.3.cloned.1.call-done = bf16[512,2048]{1,0:T(8,128)(2,1)} async-done(((bf16[128,2048]{1,0:T(8,128)(2,1)}), bf16[512,2048]{1,0:T(8,128)(2,1)}) %all-gather.3.cloned.1.call-update) | async-done | bytes 2097168 | tf_op jit(solution)/shard_map/all_gather | solution.py:42
  73.5 4.9 %fusion.11 = (bf16[512]{0:T(512)(128)(2,1)S(1)}, bf16[768,512]{1,0:T(8,128)(2,1)}, bf16[768,512]{1,0:T(8,128)(2,1)}) fusion(bf16[4,192,512]{2,1,0:T(8,128)(2,1)} %all-to-all-done, f32[512]{0:T(512)S(1)} %broadcast_multiply_fusion, f32[512]{0:T(512)S(1)} %bitcast.46, bf16[768,2048]{1,0:T(8,128)(2,1)S(1)} %bitcast.40, ...), kind=kOutput, calls=%fused_computation.18 | convolution fusion | flops 1613757952 | bytes 7607296 | tf_op jit(solution)/shard_map/dot_general | solution.py:68
  78.4 10.2 %all_to_all.21 = bf16[4,1,128]{2,1,0:T(2,128)(2,1)S(1)} all-to-all(bf16[4,1,128]{2,1,0:T(2,128)(2,1)S(1)} %copy.15), channel_id=1, replica_groups=mesh['rep'=32,'yh'=4,'x'=4] {'yh'}, dimensions={0} | all-to-all | bytes 2048 | tf_op jit(solution)/shard_map/all_to_all | solution.py:30
  88.6 4.8 %all-to-all-start.2 = ((bf16[4,192,512]{2,1,0:T(8,128)(2,1)}), bf16[4,192,512]{2,1,0:T(8,128)(2,1)S(1)}, u32[]{:S(2)}, u32[]{:S(2)}) async-start(bf16[4,192,512]{2,1,0:T(8,128)(2,1)} %bitcast.43), calls=%async_computation.2 | async-start | bytes 1572864 | tf_op jit(solution)/shard_map/all_to_all | solution.py:30
  94.1 5.3 %multiply_convert_fusion = bf16[768,2048]{1,0:T(8,128)(2,1)} fusion(bf16[768,512]{1,0:T(8,128)(2,1)} %get-tuple-element.52, bf16[512,2048]{1,0:T(8,128)(2,1)} %all-gather.3.cloned.1.call-done), kind=kOutput, calls=%fused_computation | convolution fusion | flops 1613758464 | bytes 6029312 | tf_op jit(solution)/shard_map/dot_general | solution.py:66
  99.4 2.1 %all-to-all-done.2 = bf16[4,192,512]{2,1,0:T(8,128)(2,1)S(1)} async-done(((bf16[4,192,512]{2,1,0:T(8,128)(2,1)}), bf16[4,192,512]{2,1,0:T(8,128)(2,1)S(1)}, u32[]{:S(2)}, u32[]{:S(2)}) %all-to-all-start.2) | async-done | bytes 786464 | tf_op jit(solution)/shard_map/all_to_all | solution.py:30
  101.4 7.6 %all-to-all-start.1 = ((bf16[4,192,2048]{2,1,0:T(8,128)(2,1)}), bf16[4,192,2048]{2,1,0:T(8,128)(2,1)}, u32[]{:S(2)}, u32[]{:S(2)}) async-start(bf16[4,192,2048]{2,1,0:T(8,128)(2,1)} %bitcast.4), calls=%async_computation.1 | async-start | bytes 6291456 | tf_op jit(solution)/shard_map/all_to_all | solution.py:30
  109.5 2.2 %copy.17 = f32[4,192,4,128]{3,0,2,1:T(4,128)} copy(f32[4,192,4,128]{3,2,1,0:T(4,128)S(1)} %reshape.73) | data formatting | bytes 3145728 | tf_op jit(solution)/shard_map/convert_element_type | solution.py:79
  111.7 2.0 %reshape.72 = f32[192,2048]{1,0:T(8,128)S(1)} reshape(f32[192,4,4,128]{3,2,1,0:T(4,128)} %bitcast.41) | data formatting | bytes 3145728 | tf_op jit(solution)/shard_map/convert_element_type | solution.py:79
  115.3 13.5 %reduce-scatter.2.cloned.1.call-done = bf16[128,2048]{1,0:T(8,128)(2,1)} async-done(((bf16[512,2048]{1,0:T(8,128)(2,1)}), bf16[128,2048]{1,0:T(8,128)(2,1)}) %reduce-scatter.2.cloned.1.call-update) | async-done | bytes 524304 | tf_op jit(solution)/shard_map/reduce_scatter | solution.py:63
  130.0 29.8 %conditional.4 = (bf16[128,2048]{1,0:T(8,128)(2,1)}, bf16[128]{0:T(256)(128)(2,1)}) conditional(s32[]{:T(128)} %clamp.3, (bf16[128,2048]{1,0:T(8,128)(2,1)S(1)}, bf16[128]{0:T(256)(128)(2,1)S(1)}) %tuple.50, (bf16[128,2048]{1,0:T(8,128)(2,1)S(1)}, bf16[128]{0:T(256)(128)(2,1)S(1)}) %tuple.50, ...), branch_computations={%region_6.7_spmd, %region_7.8_spmd, %region_8.9_spmd, %region_9.10... | conditional | bytes 2098272
  130.0 4.7 %collective-permute-start.4 = (bf16[128,2048]{1,0:T(8,128)(2,1)S(1)}, bf16[128,2048]{1,0:T(8,128)(2,1)}, u32[]{:S(2)}, u32[]{:S(2)}) collective-permute-start(bf16[128,2048]{1,0:T(8,128)(2,1)S(1)} %get-tuple-element.32), channel_id=1, source_target_pairs={{0,64},{16,80},{32,96},{48,112},{64,128},{80,144},{96,160},{112,17... | collective-permute-start | bytes 1572872 | tf_op jit(solution)/shard_map/cond/branch_2_fun/ppermute | solution.py:19
  134.7 6.0 %collective-permute-start.5 = (bf16[128]{0:T(256)(128)(2,1)S(1)}, bf16[128]{0:T(256)(128)(2,1)}, u32[]{:S(2)}, u32[]{:S(2)}) collective-permute-start(bf16[128]{0:T(256)(128)(2,1)S(1)} %get-tuple-element.33), channel_id=1, source_target_pairs={{0,64},{16,80},{32,96},{48,112},{64,128},{80,144},{96,160},{112,17... | collective-permute-start | bytes 776 | tf_op jit(solution)/shard_map/cond/branch_2_fun/ppermute | solution.py:19
  140.7 19.1 %collective-permute-done.5 = bf16[128]{0:T(256)(128)(2,1)} collective-permute-done((bf16[128]{0:T(256)(128)(2,1)S(1)}, bf16[128]{0:T(256)(128)(2,1)}, u32[]{:S(2)}, u32[]{:S(2)}) %collective-permute-start.5) | collective-permute-done | bytes 288 | tf_op jit(solution)/shard_map/cond/branch_2_fun/ppermute | solution.py:19
  160.9 2.0 %fusion.13 = bf16[128,2048]{1,0:T(8,128)(2,1)} fusion(bf16[128,2048]{1,0:T(8,128)(2,1)} %get-tuple-element.48, bf16[128,2048]{1,0:T(8,128)(2,1)S(1)} %subtract_convert_fusion), kind=kLoop, calls=%fused_computation.23 | loop fusion | flops 1310720 | bytes 1572864 | tf_op jit(solution)/shard_map/convert_element_type | solution.py:92
  162.9 3.6 %reduce_sum.49 = bf16[192,2048]{1,0:T(8,128)(2,1)} reduce(bf16[4,192,2048]{2,1,0:T(8,128)(2,1)} %all-to-all-done.1, bf16[]{:T(256)} %constant.53.clone.1), dimensions={0}, to_apply=%region_1.2 | reduce | flops 1179648 | bytes 3932162 | tf_op jit(solution)/shard_map/reduce_sum | solution.py:77
  (36 shorter events, 14.5 us)
Async XLA Ops:
  7.2 66.4 %all-gather.3.cloned.1.call-start = ((), (), s32[]{:S(2)}) async-start(), calls=%async_computation.5 | async-start | bytes 2621440 | tf_op jit(solution)/shard_map/all_gather | solution.py:42
  7.2 39.0 %collective-permute-start.8 = (bf16[192,2048]{1,0:T(8,128)(2,1)}, bf16[192,2048]{1,0:T(8,128)(2,1)}, u32[]{:S(2)}, u32[]{:S(2)}) collective-permute-start(bf16[192,2048]{1,0:T(8,128)(2,1)} %param.12), channel_id=1, source_target_pairs={{0,1},{1,2},{2,3},{3,0},{4,5},{5,6},{6,7},{7,4},{8,9},{9,10},{10,1... | collective-permute-start | bytes 2359304 | tf_op jit(solution)/shard_map/ppermute | solution.py:19
  10.3 37.1 %collective-permute-start.9 = (bf16[192,2048]{1,0:T(8,128)(2,1)}, bf16[192,2048]{1,0:T(8,128)(2,1)}, u32[]{:S(2)}, u32[]{:S(2)}) collective-permute-start(bf16[192,2048]{1,0:T(8,128)(2,1)} %param.12), channel_id=1, source_target_pairs={{0,3},{1,0},{2,1},{3,2},{4,7},{5,4},{6,5},{7,6},{8,11},{9,8},{10,9... | collective-permute-start | bytes 2359304 | tf_op jit(solution)/shard_map/ppermute | solution.py:19
  13.1 35.6 %collective-permute-start.10 = (bf16[192,2048]{1,0:T(8,128)(2,1)}, bf16[192,2048]{1,0:T(8,128)(2,1)}, u32[]{:S(2)}, u32[]{:S(2)}) collective-permute-start(bf16[192,2048]{1,0:T(8,128)(2,1)} %param.12), channel_id=1, source_target_pairs={{0,2},{1,3},{2,0},{3,1},{4,6},{5,7},{6,4},{7,5},{8,10},{9,11},{10,... | collective-permute-start | bytes 2359304 | tf_op jit(solution)/shard_map/ppermute | solution.py:19
  20.0 7.5 %copy-start.2 = (bf16[128]{0:T(256)(128)(2,1)S(1)}, bf16[128]{0:T(256)(128)(2,1)}, u32[]{:S(2)}) copy-start(bf16[128]{0:T(256)(128)(2,1)} %param.11) | copy-start | bytes 772
  21.5 32.6 %all-to-all-start = ((bf16[4,192,512]{2,1,0:T(8,128)(2,1)}), bf16[4,192,512]{2,1,0:T(8,128)(2,1)}, u32[]{:S(2)}, u32[]{:S(2)}) async-start(bf16[4,192,512]{2,1,0:T(8,128)(2,1)} %reshape.67), calls=%async_computation | async-start | bytes 1572864 | tf_op jit(solution)/shard_map/all_to_all | solution.py:30
  27.5 101.3 %reduce-scatter.2.cloned.1.call-start = ((), (), s32[]{:S(2)}) async-start(), calls=%async_computation.6 | async-start | bytes 2621440 | tf_op jit(solution)/shard_map/reduce_scatter | solution.py:63
  88.6 12.9 %all-to-all-start.2 = ((bf16[4,192,512]{2,1,0:T(8,128)(2,1)}), bf16[4,192,512]{2,1,0:T(8,128)(2,1)S(1)}, u32[]{:S(2)}, u32[]{:S(2)}) async-start(bf16[4,192,512]{2,1,0:T(8,128)(2,1)} %bitcast.43), calls=%async_computation.2 | async-start | bytes 1572864 | tf_op jit(solution)/shard_map/all_to_all | solution.py:30
  101.4 61.5 %all-to-all-start.1 = ((bf16[4,192,2048]{2,1,0:T(8,128)(2,1)}), bf16[4,192,2048]{2,1,0:T(8,128)(2,1)}, u32[]{:S(2)}, u32[]{:S(2)}) async-start(bf16[4,192,2048]{2,1,0:T(8,128)(2,1)} %bitcast.4), calls=%async_computation.1 | async-start | bytes 6291456 | tf_op jit(solution)/shard_map/all_to_all | solution.py:30
  111.7 2.0 %copy-start = (bf16[192,2048]{1,0:T(8,128)(2,1)S(1)}, bf16[192,2048]{1,0:T(8,128)(2,1)}, u32[]{:S(2)}) copy-start(bf16[192,2048]{1,0:T(8,128)(2,1)} %param.9) | copy-start | bytes 2359300
  114.1 14.7 %copy-start.1 = (bf16[128,2048]{1,0:T(8,128)(2,1)S(1)}, bf16[128,2048]{1,0:T(8,128)(2,1)}, u32[]{:S(2)}) copy-start(bf16[128,2048]{1,0:T(8,128)(2,1)} %param.10) | copy-start | bytes 1572868
  130.0 29.8 %collective-permute-start.4 = (bf16[128,2048]{1,0:T(8,128)(2,1)S(1)}, bf16[128,2048]{1,0:T(8,128)(2,1)}, u32[]{:S(2)}, u32[]{:S(2)}) collective-permute-start(bf16[128,2048]{1,0:T(8,128)(2,1)S(1)} %get-tuple-element.32), channel_id=1, source_target_pairs={{0,64},{16,80},{32,96},{48,112},{64,128},{80,144},{96,160},{112,17... | collective-permute-start | bytes 1572872 | tf_op jit(solution)/shard_map/cond/branch_2_fun/ppermute | solution.py:19
  134.7 25.1 %collective-permute-start.5 = (bf16[128]{0:T(256)(128)(2,1)S(1)}, bf16[128]{0:T(256)(128)(2,1)}, u32[]{:S(2)}, u32[]{:S(2)}) collective-permute-start(bf16[128]{0:T(256)(128)(2,1)S(1)} %get-tuple-element.33), channel_id=1, source_target_pairs={{0,64},{16,80},{32,96},{48,112},{64,128},{80,144},{96,160},{112,17... | collective-permute-start | bytes 776 | tf_op jit(solution)/shard_map/cond/branch_2_fun/ppermute | solution.py:19
Sparse Core Ops, SparseCore 0:
  16.9 56.6 all-gather.2
  76.4 52.3 reduce-scatter.1

commit v2 on v1

v2 whole, which is shorter than its diff:
```python
import functools
import math

import jax
import jax.numpy as jnp
from jax import lax
from jax.experimental import pallas as pl
from jax.experimental.pallas import tpu as pltpu
from jax.sharding import Mesh
from jax.sharding import PartitionSpec as P

eps = 1e-05
step_rate = 0.75
gain_rate = 0.004
F32 = jnp.float32
BF16 = jnp.bfloat16
VMEM_LIMIT = 32 * 1024 * 1024
ANY = pl.BlockSpec(memory_space=pl.ANY)
BLOCK = None
SCALAR = pl.BlockSpec(memory_space=pltpu.SMEM)


def array(shape, dtype=BF16):
    return jax.ShapeDtypeStruct(shape, dtype)


def in_hbm(shape, dtype=BF16):
    return pltpu.HBM(shape, dtype)


def call(kernel, ins, outs, scratch=(), flops=0, moved=0):
    values = [
        v if spec is SCALAR else pltpu.with_memory_space_constraint(v, pltpu.HBM) for v, spec in ins
    ]
    return pl.pallas_call(
        kernel,
        grid=(1,),
        out_shape=list(outs),
        in_specs=[whole(v.shape) if spec is BLOCK else spec for v, spec in ins],
        out_specs=[whole(shape.shape) for shape in outs],
        scratch_shapes=list(scratch),
        compiler_params=pltpu.CompilerParams(vmem_limit_bytes=VMEM_LIMIT),
        cost_estimate=pl.CostEstimate(flops=flops, bytes_accessed=moved, transcendentals=0),
    )(*values)


def whole(shape):
    return pl.BlockSpec(shape, lambda s: (0,) * len(shape))


def fetch(pairs, sems):
    copies = [pltpu.make_async_copy(src, dst, sems.at[i]) for i, (src, dst) in enumerate(pairs)]
    for copy in copies:
        copy.start()
    return copies


def shifted(value, axis, steps):
    count = lax.axis_size(axis)
    pairs = [(source, (source + steps) % count) for source in range(count)]
    return lax.ppermute(value, axis, pairs)


def exchange(blocks, axis):
    return lax.all_to_all(blocks, axis, split_axis=0, concat_axis=0, tiled=True)


def column_of(row):
    n = row.shape[1]
    down = lax.broadcasted_iota(jnp.int32, (n, n), 0)
    along = lax.broadcasted_iota(jnp.int32, (n, n), 1)
    return jnp.sum(jnp.where(down == along, row, 0.0), axis=1, keepdims=True)


def row_of(column):
    n = column.shape[0]
    down = lax.broadcasted_iota(jnp.int32, (n, n), 0)
    along = lax.broadcasted_iota(jnp.int32, (n, n), 1)
    return jnp.sum(jnp.where(down == along, column, 0.0), axis=0, keepdims=True)


def weight_kernel(weight_ref, gain_ref, out_ref):
    scaled = (weight_ref[...].astype(F32) * column_of(gain_ref[...].astype(F32))).astype(BF16)
    for i in range(out_ref.shape[0]):
        out_ref[i] = scaled


def token_kernel(
    n_x, me_ref, tok_ref, up_ref, dep_ref, own_ref, sa_ref, sb_ref, ta_ref, tb_ref, rstd_ref
):
    me = me_ref[0]
    width, part = tok_ref.shape[1], own_ref.shape[1]
    rows = part // (width // part)
    half, quarter = width // 2, part // 2
    for d in range(n_x):
        slot = lax.rem(me + d, n_x) * rows
        for k in range(part // rows):
            block = tok_ref[:, pl.ds(pl.multiple_of(slot + k * n_x * rows, rows), rows)]
            at = k * rows
            if d == 0:
                own_ref[:, at : at + rows] = block
            elif d == 1:
                ta_ref[:, half + at : half + at + rows] = block
            elif d == 3:
                tb_ref[:, half + at : half + at + rows] = block
            elif at < quarter:
                sa_ref[:, half + at : half + at + rows] = block
            else:
                sb_ref[:, half + at - quarter : half + at - quarter + rows] = block
    x = tok_ref[...].astype(F32)
    rstd = lax.rsqrt(jnp.mean(x * x, axis=1, keepdims=True) + eps)
    rstd_ref[...] = jnp.broadcast_to(rstd, rstd_ref.shape)
    up_a = (up_ref[:, :half].astype(F32) * rstd).astype(BF16)
    up_b = (up_ref[:, half:].astype(F32) * rstd).astype(BF16)
    sa_ref[:, :half] = up_a
    tb_ref[:, :half] = up_a
    sb_ref[:, :half] = up_b
    ta_ref[:, :half] = up_b


def grad_kernel(scale, xo, lt, rt, fa, fb, sa, la, sb, rb, out, *scratch):
    (vx, vlt, vrt, vfa, vfb, vsa, vla, vsb, vrb), turned, sems = scratch[:9], scratch[9], scratch[10]
    half = vsa.shape[1]
    rows = out.shape[1]
    tile = 256
    copies = fetch(
        [
            (xo, vx),
            (lt, vlt),
            (rt, vrt),
            (fa, vfa),
            (fb, vfb),
            (sa.at[:, :half], vsa),
            (la.at[:, :half], vla),
            (sb.at[:, :half], vsb),
            (rb.at[:, :half], vrb),
        ],
        sems,
    )
    for copy in copies[:5]:
        copy.wait()
    far = jnp.concatenate([vfa[:, half:], vfb[:, half:]], axis=1)
    turned[...] = jnp.concatenate([vx[...], vlt[:, half:], vrt[:, half:], far], axis=0).T
    for h, refs in enumerate(((vsa, vla, vrt, vfa), (vsb, vlt, vrb, vfb))):
        for copy in copies[5 + 2 * h : 7 + 2 * h]:
            copy.wait()

        @pl.loop(0, half // tile)
        def _(j):
            cols = pl.ds(pl.multiple_of(j * tile, tile), tile)
            block = jnp.concatenate([r[:, cols] for r in refs], axis=0)
            total = jnp.dot(turned[...], block, preferred_element_type=F32) * scale
            to = pl.ds(pl.multiple_of(h * half + j * tile, tile), tile)
            for k in range(out.shape[0]):
                out[k, :, to] = total[k * rows : (k + 1) * rows].astype(BF16)


def times_turned(left, right):
    return lax.dot_general(left, right, (((1,), (1,)), ((), ())), preferred_element_type=F32)


def far_kernel(scale, fa, fb, w, dep, out_a, out_b, vfa, vfb, vw, sems):
    part, width = vw.shape
    half, quarter = width // 2, part // 2
    copies = fetch(
        [
            (fa, vfa),
            (fb, vfb),
            (w.at[:, :half], vw.at[:, :half]),
            (w.at[:, half:], vw.at[:, half:]),
        ],
        sems,
    )
    copies[0].wait()
    copies[1].wait()
    x = jnp.concatenate([vfa[:, half:], vfb[:, half:]], axis=1)
    g = 0.0
    for h, (u, out) in enumerate(((vfa, out_a), (vfb, out_b))):
        copies[2 + h].wait()
        block = vw[:, h * half : (h + 1) * half]
        out[:, :half] = (jnp.dot(x, block, preferred_element_type=F32) * scale).astype(BF16)
        g = g + times_turned(u[:, :half], block)
    g = (g * scale).astype(BF16)
    out_a[:, half:] = g[:, :quarter]
    out_b[:, half:] = g[:, quarter:]


def near_kernel(
    scale, xo, lt, rt, w, sa, la, sb, rb, dep, p0, g0, tr, tl, pr, pl_, vx, vlt, vrt, vw, vsa, vla, vsb, vrb, sems
):
    part, width = vw.shape
    count, half = vsa.shape
    tile = half // 2
    copies = fetch(
        [
            (xo, vx),
            (lt, vlt),
            (rt, vrt),
            (w.at[:, :half], vw.at[:, :half]),
            (w.at[:, half:], vw.at[:, half:]),
            (sa.at[:, :half], vsa),
            (la.at[:, :half], vla),
            (sb.at[:, :half], vsb),
            (rb.at[:, :half], vrb),
        ],
        sems,
    )
    for copy in copies[:3]:
        copy.wait()
    x = jnp.concatenate([vx[...], vlt[:, half:], vrt[:, half:]], axis=0)
    for h in range(2):
        copies[3 + h].wait()
        for t in range(2):
            at = h * half + t * tile
            cols = slice(t * tile, (t + 1) * tile)
            p = jnp.dot(x, vw[:, at : at + tile], preferred_element_type=F32) * scale
            p0[:, at : at + tile] = p[:count]
            if h == 0:
                tl[:, cols] = p[count : 2 * count].astype(BF16)
                pr[:, cols] = p[2 * count :]
            else:
                tr[:, cols] = p[2 * count :].astype(BF16)
                pl_[:, cols] = p[count : 2 * count]
    for copy in copies[5:]:
        copy.wait()
    up_a = jnp.concatenate([vsa[...], vla[...], vrt[:, :half]], axis=0)
    up_b = jnp.concatenate([vsb[...], vlt[:, :half], vrb[...]], axis=0)
    for k in range(0, part, 256):
        g = times_turned(up_a, vw[k : k + 256, :half]) + times_turned(up_b, vw[k : k + 256, half:])
        g = (g * scale).astype(BF16)
        g0[:, k : k + 256] = g[:count]
        tl[:, half + k : half + k + 256] = g[count : 2 * count]
        tr[:, half + k : half + k + 256] = g[2 * count :]


def pass_kernel(pr, pl_, in_a, in_b, dr, dl):
    half = pr.shape[1]
    dr[:, :half] = (pr[...] + in_a[:, :half].astype(F32)).astype(BF16)
    dr[:, half:] = in_a[:, half:]
    dl[:, :half] = (pl_[...] + in_b[:, :half].astype(F32)).astype(BF16)
    dl[:, half:] = in_b[:, half:]


def result_kernel(n_x, me_ref, tok_ref, rstd_ref, p0, g0, lt, ld, rt, rd, out_p, out_x, back):
    me = me_ref[0]
    width, part = tok_ref.shape[1], g0.shape[1]
    rows = part // (width // part)
    half, quarter = width // 2, part // 2
    rstd = rstd_ref[:, :1]
    for h, (l, r) in enumerate(((ld, rt), (lt, rd))):
        cols = slice(h * half, (h + 1) * half)
        total = p0[:, cols] + l[:, :half].astype(F32) + r[:, :half].astype(F32)
        out_p[:, cols] = (total * rstd).astype(BF16)
    for d in range(n_x):
        slot = lax.rem(me + d, n_x) * rows
        for k in range(part // rows):
            at = k * rows
            if d == 0:
                block = g0[:, at : at + rows]
            elif d == 1:
                block = rt[:, half + at : half + at + rows]
            elif d == 3:
                block = lt[:, half + at : half + at + rows]
            elif at < quarter:
                block = ld[:, half + at : half + at + rows]
            else:
                block = rd[:, half + at - quarter : half + at - quarter + rows]
            back[:, pl.ds(pl.multiple_of(slot + k * n_x * rows, rows), rows)] = block.astype(F32)
    g = back[...]
    xhat = tok_ref[...].astype(F32) * rstd
    mean = jnp.mean(g * xhat, axis=1, keepdims=True)
    out_x[...] = (g - xhat * mean).astype(BF16)


def step_kernel(parts_ref, weight_ref, gain_ref, dep_1, dep_2, out_w_ref, out_g_ref):
    gain = gain_ref[...].astype(F32)
    grad = jnp.sum(parts_ref[...].astype(F32), axis=0)
    w = weight_ref[...].astype(F32)
    slope = jnp.sum(grad * w, axis=1, keepdims=True)
    out_w_ref[...] = (w - step_rate * (column_of(gain) * grad)).astype(BF16)
    out_g_ref[...] = (gain - gain_rate * row_of(slope)).astype(BF16)


def mean_kernel(w_ref, pw_ref, g_ref, pg_ref, out_w_ref, out_g_ref):
    out_w_ref[...] = (0.5 * (w_ref[...].astype(F32) + pw_ref[...].astype(F32))).astype(BF16)
    out_g_ref[...] = (0.5 * (g_ref[...].astype(F32) + pg_ref[...].astype(F32))).astype(BF16)


def on_device(tokens, weight, gain, upstream, step):
    n_x, n_y = lax.axis_size("x"), lax.axis_size("yh")
    rows, width_out = weight.shape
    count, width_in = tokens.shape
    scale = 1.0 / math.sqrt(width_in)
    half = width_out // 2
    part = n_y * rows
    me = lax.axis_index("x").astype(jnp.int32).reshape(1)
    gain_row = gain.reshape(1, rows)
    flops = 2 * n_x * count * part * width_out
    moved = 2 * (n_x * count * (part + width_out) + part * width_out)
    quarter = part // 2
    vmem = lambda *shape: pltpu.VMEM(shape, BF16)
    sems = lambda n: pltpu.SemaphoreType.DMA((n,))
    short, long = in_hbm((count, half + quarter)), in_hbm((count, half + part))

    (copies,) = call(
        weight_kernel,
        [(weight, BLOCK), (gain_row, BLOCK)],
        [in_hbm((n_y, rows, width_out))],
    )
    full_weight = exchange(copies, "yh").reshape(part, width_out)

    x_own, sa, sb, ta, tb, rstd = call(
        functools.partial(token_kernel, n_x),
        [(me, SCALAR), (tokens, BLOCK), (upstream, BLOCK), (copies, ANY)],
        [in_hbm((count, part)), short, short, long, long, in_hbm((count, 128), F32)],
    )
    la, rb = shifted(sa, "x", 1), shifted(sb, "x", -1)
    lt, rt = shifted(ta, "x", 1), shifted(tb, "x", -1)
    fa, fb = shifted(la, "x", 1), shifted(rb, "x", -1)

    (part_w,) = call(
        functools.partial(grad_kernel, scale),
        [(v, ANY) for v in (x_own, lt, rt, fa, fb, sa, la, sb, rb)],
        [in_hbm((n_y, rows, width_out))],
        [vmem(count, part)]
        + [vmem(count, half + part)] * 2
        + [vmem(count, half + quarter)] * 2
        + [vmem(count, half)] * 4
        + [vmem(part, n_x * count), sems(9)],
        flops,
        moved,
    )
    pieces_w = exchange(part_w, "yh")

    out_a, out_b = call(
        functools.partial(far_kernel, scale),
        [(v, ANY) for v in (fa, fb, full_weight, part_w)],
        [short, short],
        [vmem(count, half + quarter)] * 2 + [vmem(part, width_out), sems(4)],
        flops // 2,
        moved // 2,
    )
    in_a, in_b = shifted(out_a, "x", 1), shifted(out_b, "x", -1)
    p0, g0, tr, tl, pr, pl_ = call(
        functools.partial(near_kernel, scale),
        [(v, ANY) for v in (x_own, lt, rt, full_weight, sa, la, sb, rb, out_a)],
        [in_hbm((count, width_out), F32), in_hbm((count, part)), long, long]
        + [in_hbm((count, half), F32)] * 2,
        [vmem(count, part)]
        + [vmem(count, half + part)] * 2
        + [vmem(part, width_out)]
        + [vmem(count, half)] * 4
        + [sems(9)],
        2 * flops,
        2 * moved,
    )
    got_lt, got_rt = shifted(tr, "x", 1), shifted(tl, "x", -1)
    dr, dl = call(
        pass_kernel,
        [(pr, BLOCK), (pl_, BLOCK), (in_a, BLOCK), (in_b, BLOCK)],
        [short, short],
        moved=moved,
    )
    got_ld, got_rd = shifted(dr, "x", 1), shifted(dl, "x", -1)

    stepped_w, stepped_g = call(
        step_kernel,
        [(pieces_w, BLOCK), (weight, BLOCK), (gain_row, BLOCK), (got_ld, ANY), (got_rd, ANY)],
        [in_hbm((rows, width_out)), in_hbm((1, rows))],
        moved=moved,
    )

    def gossip(distance):
        def branch(params, rest):
            peers = jax.tree.map(lambda part: shifted(part, "rep", distance), params)
            results = call(
                functools.partial(result_kernel, n_x),
                [(rest[0], SCALAR)] + [(v, BLOCK) for v in rest[1:]],
                [in_hbm((count, width_out)), in_hbm((count, width_in))],
                [pltpu.VMEM((count, width_in), F32)],
                moved=moved,
            )
            return peers, results

        return branch

    (peer_w, peer_g), (projected, input_gradient) = lax.switch(
        step[0] % 4,
        [gossip(distance) for distance in (1, 2, 4, 8)],
        (stepped_w, stepped_g),
        (me, tokens, rstd, p0, g0, got_lt, got_ld, got_rt, got_rd),
    )
    new_weight, new_gain = call(
        mean_kernel,
        [(stepped_w, BLOCK), (peer_w, BLOCK), (stepped_g, BLOCK), (peer_g, BLOCK)],
        [in_hbm((rows, width_out)), in_hbm((1, rows))],
    )
    return (projected, input_gradient, new_weight, new_gain.reshape(rows))


def solution(mesh):
    n_rep, n_fsdp = mesh.devices.shape
    n_x = 4
    split = Mesh(mesh.devices.reshape(n_rep, n_fsdp // n_x, n_x), ("rep", "yh", "x"))
    every = ("rep", "yh", "x")
    placed = (P(every, None), P(every, None), P(every), P(every, None), P())
    return jax.shard_map(
        on_device,
        mesh=split,
        in_specs=placed,
        out_specs=(P(every, None), P(every, None), P(every, None), P(every)),
        check_vma=False,
    )
```

time: 174 us -> 142 us (0.82)
  the two profiles are of different devices: /device:TPU:60 before, /device:TPU:30 now
where the time goes in v2:
time: 142 us
  starting transfers between devices  56.6 us (40%)
  waiting for transfers between devices  43.3 us (30%)
  Pallas kernels  35.1 us (25%)
  local copies, waits for them, and re-layouts  5.12 us (4%)
  between operations  1.51 us (1%)
    ppermute x14, waiting for transfers between devices, shifted(): return lax.ppermute(value, axis, pairs)  43.3 us
    ppermute x14, starting transfers between devices, shifted(): return lax.ppermute(value, axis, pairs)  42.9 us
    pallas_call x9, Pallas kernels, call(): pl.pallas_call(kernel, grid=(1,), out_shape=list(outs), in_specs=[whole(v...  35.1 us
    all_to_all x2, starting transfers between devices, exchange(): return lax.all_to_all(blocks, axis, split_axis=0, concat_axis=0, tiled=True)  13.7 us
    unnamed x24, local copies, waits for them, and re-layouts  5.12 us
  transfers between devices with their start and end apart: 16, of which 8 were waited for; matrix products, arithmetic and copies ran while one was open for 0% of the time, Pallas kernels for 21%

profile of v2, /device:TPU:30, one launch (start us, length us, event | category | flops | bytes accessed | tf_op | source)
XLA Modules:
  0.0 141.6 jit_solution(3718943530214604440)
XLA Ops:
  3.2 6.5 %all-to-all-start.1 = ((bf16[4,128,2048]{2,1,0:T(8,128)(2,1)}), bf16[4,128,2048]{2,1,0:T(8,128)(2,1)S(1)}, u32[]{:S(2)}, u32[]{:S(2)}) async-start(bf16[4,128,2048]{2,1,0:T(8,128)(2,1)} %shard_map.84.dep_ref), calls=%async_computation.1 | async-start | bytes 4194304 | tf_op jit(solution)/shard_map/all_to_all | solution.py:65
  9.7 3.2 %shard_map.85 = (bf16[192,512]{1,0:T(8,128)(2,1)}, bf16[192,1280]{1,0:T(8,128)(2,1)}, bf16[192,1280]{1,0:T(8,128)(2,1)}, bf16[192,1536]{1,0:T(8,128)(2,1)}, bf16...) custom-call(s32[1]{0:T(128)} %bitcast.1.me_ref, bf16[192,2048]{1,0:T(8,128)(2,1)} %tok_ref.1, bf16[192,2048]{1,0:T(8,128)(2,1)} %up_ref.1, ...), custom_call_target="tpu_custom_call" | custom-call | tf_op jit(solution)/shard_map/pallas_call | solution.py:35
  15.4 3.5 %collective-permute-start.12 = (bf16[192,1280]{1,0:T(8,128)(2,1)}, bf16[192,1280]{1,0:T(8,128)(2,1)S(1)}, u32[]{:S(2)}, u32[]{:S(2)}) collective-permute-start(bf16[192,1280]{1,0:T(8,128)(2,1)} %get-tuple-element.172.sb), channel_id=1, source_target_pairs={{0,3},{1,0},{2,1},{3,2},{4,7},{5,4},{6,5},{7,6},{8,11},{9,8},{10,9... | collective-permute-start | bytes 1474568 | tf_op jit(solution)/shard_map/ppermute | solution.py:61
  18.8 3.6 %collective-permute-start.8 = (bf16[192,1536]{1,0:T(8,128)(2,1)}, bf16[192,1536]{1,0:T(8,128)(2,1)S(1)}, u32[]{:S(2)}, u32[]{:S(2)}) collective-permute-start(bf16[192,1536]{1,0:T(8,128)(2,1)} %get-tuple-element.169), channel_id=1, source_target_pairs={{0,1},{1,2},{2,3},{3,0},{4,5},{5,6},{6,7},{7,4},{8,9},{9,10},{10,1... | collective-permute-start | bytes 1769480 | tf_op jit(solution)/shard_map/ppermute | solution.py:61
  24.7 4.6 %collective-permute-done.10.la = bf16[192,1280]{1,0:T(8,128)(2,1)S(1)} collective-permute-done((bf16[192,1280]{1,0:T(8,128)(2,1)}, bf16[192,1280]{1,0:T(8,128)(2,1)S(1)}, u32[]{:S(2)}, u32[]{:S(2)}) %collective-permute-start.10) | collective-permute-done | bytes 491552 | tf_op jit(solution)/shard_map/ppermute | solution.py:61
  29.2 3.6 %collective-permute-start.11 = (bf16[192,1280]{1,0:T(8,128)(2,1)S(1)}, bf16[192,1280]{1,0:T(8,128)(2,1)S(1)}, u32[]{:S(2)}, u32[]{:S(2)}) collective-permute-start(bf16[192,1280]{1,0:T(8,128)(2,1)S(1)} %collective-permute-done.10.la), channel_id=1, source_target_pairs={{0,1},{1,2},{2,3},{3,0},{4,5},{5,6},{6,7},{7,4},{8,9},{9,10},{10,1... | collective-permute-start | bytes 1474568 | tf_op jit(solution)/shard_map/ppermute | solution.py:61
  35.1 6.8 %collective-permute-done.8.lt = bf16[192,1536]{1,0:T(8,128)(2,1)S(1)} collective-permute-done((bf16[192,1536]{1,0:T(8,128)(2,1)}, bf16[192,1536]{1,0:T(8,128)(2,1)S(1)}, u32[]{:S(2)}, u32[]{:S(2)}) %collective-permute-start.8) | collective-permute-done | bytes 589856 | tf_op jit(solution)/shard_map/ppermute | solution.py:61
  41.9 3.6 %collective-permute-done.9.rt = bf16[192,1536]{1,0:T(8,128)(2,1)S(1)} collective-permute-done((bf16[192,1536]{1,0:T(8,128)(2,1)}, bf16[192,1536]{1,0:T(8,128)(2,1)S(1)}, u32[]{:S(2)}, u32[]{:S(2)}) %collective-permute-start.9) | collective-permute-done | bytes 589856 | tf_op jit(solution)/shard_map/ppermute | solution.py:61
  45.5 5.2 %collective-permute-done.11.fa = bf16[192,1280]{1,0:T(8,128)(2,1)S(1)} collective-permute-done((bf16[192,1280]{1,0:T(8,128)(2,1)S(1)}, bf16[192,1280]{1,0:T(8,128)(2,1)S(1)}, u32[]{:S(2)}, u32[]{:S(2)}) %collective-permute-start.11) | collective-permute-done | bytes 491552 | tf_op jit(solution)/shard_map/ppermute | solution.py:61
  50.6 3.3 %collective-permute-done.13.fb = bf16[192,1280]{1,0:T(8,128)(2,1)S(1)} collective-permute-done((bf16[192,1280]{1,0:T(8,128)(2,1)S(1)}, bf16[192,1280]{1,0:T(8,128)(2,1)S(1)}, u32[]{:S(2)}, u32[]{:S(2)}) %collective-permute-start.13) | collective-permute-done | bytes 491552 | tf_op jit(solution)/shard_map/ppermute | solution.py:61
  54.7 6.4 %shard_map.86.dep = bf16[4,128,2048]{2,1,0:T(8,128)(2,1)} custom-call(bf16[192,512]{1,0:T(8,128)(2,1)} %get-tuple-element.168.xo, bf16[192,1536]{1,0:T(8,128)(2,1)} %copy-done.6, bf16[192,1536]{1,0:T(8,128)(2,1)} %copy-done.7, bf16[192,1280]{1,0:T(8,128)(2,1)} %copy-done.4, bf16[192,1280]{1,0:T(8,128)(2,1)} %copy-done.5, ...), custom_call_target="tpu_custom_call" | custom-call | flops 1610612736 | bytes 6029312 | tf_op jit(solution)/shard_map/pallas_call | solution.py:35
  62.5 7.2 %all-to-all-start = ((bf16[4,128,2048]{2,1,0:T(8,128)(2,1)}), bf16[4,128,2048]{2,1,0:T(8,128)(2,1)S(1)}, u32[]{:S(2)}, u32[]{:S(2)}) async-start(bf16[4,128,2048]{2,1,0:T(8,128)(2,1)} %shard_map.86.dep), calls=%async_computation | async-start | bytes 4194304 | tf_op jit(solution)/shard_map/all_to_all | solution.py:65
  69.7 4.0 %shard_map.87 = (bf16[192,1280]{1,0:T(8,128)(2,1)}, bf16[192,1280]{1,0:T(8,128)(2,1)}) custom-call(bf16[192,1280]{1,0:T(8,128)(2,1)} %copy-done.4, bf16[192,1280]{1,0:T(8,128)(2,1)} %copy-done.5, bf16[512,2048]{1,0:T(8,128)(2,1)} %bitcast.8, bf16[4,128,2048]{2,1,0:T(8,128)(2,1)} %shard_map.86.dep), custom_call_target="tpu_custom_call" | custom-call | flops 805306368 | bytes 3014656 | tf_op jit(solution)/shard_map/pallas_call | solution.py:35
  75.9 3.7 %collective-permute-start.15 = (bf16[192,1280]{1,0:T(8,128)(2,1)}, bf16[192,1280]{1,0:T(8,128)(2,1)S(1)}, u32[]{:S(2)}, u32[]{:S(2)}) collective-permute-start(bf16[192,1280]{1,0:T(8,128)(2,1)} %get-tuple-element.176), channel_id=1, source_target_pairs={{0,3},{1,0},{2,1},{3,2},{4,7},{5,4},{6,5},{7,6},{8,11},{9,8},{10,9... | collective-permute-start | bytes 1474568 | tf_op jit(solution)/shard_map/ppermute | solution.py:61
  79.5 6.3 %shard_map.88 = (f32[192,2048]{1,0:T(8,128)}, bf16[192,512]{1,0:T(8,128)(2,1)}, bf16[192,1536]{1,0:T(8,128)(2,1)}, bf16[192,1536]{1,0:T(8,128)(2,1)}, f32[192,1024]{1,0:T(8,128)}, /*index=5*/f32[192,1024]{1,0:T(8,128)}) custom-call(bf16[192,512]{1,0:T(8,128)(2,1)} %get-tuple-element.168.xo, bf16[192,1536]{1,0:T(8,128)(2,1)} %copy-done.6, ...), custom_call_target="tpu_custom_call" | custom-call | flops 3221225472 | bytes 12058624 | tf_op jit(solution)/shard_map/pallas_call | solution.py:35
  85.8 3.4 %collective-permute-start.18 = (bf16[192,1536]{1,0:T(8,128)(2,1)}, bf16[192,1536]{1,0:T(8,128)(2,1)}, u32[]{:S(2)}, u32[]{:S(2)}) collective-permute-start(bf16[192,1536]{1,0:T(8,128)(2,1)} %get-tuple-element.184), channel_id=1, source_target_pairs={{0,1},{1,2},{2,3},{3,0},{4,5},{5,6},{6,7},{7,4},{8,9},{9,10},{10,1... | collective-permute-start | bytes 1769480 | tf_op jit(solution)/shard_map/ppermute | solution.py:61
  95.4 4.6 %collective-permute-start.16 = (bf16[192,1280]{1,0:T(8,128)(2,1)}, bf16[192,1280]{1,0:T(8,128)(2,1)S(1)}, u32[]{:S(2)}, u32[]{:S(2)}) collective-permute-start(bf16[192,1280]{1,0:T(8,128)(2,1)} %get-tuple-element.177), channel_id=1, source_target_pairs={{0,1},{1,2},{2,3},{3,0},{4,5},{5,6},{6,7},{7,4},{8,9},{9,10},{10,1... | collective-permute-start | bytes 1474568 | tf_op jit(solution)/shard_map/ppermute | solution.py:61
  102.6 8.1 %collective-permute-done.16.dep_1 = bf16[192,1280]{1,0:T(8,128)(2,1)S(1)} collective-permute-done((bf16[192,1280]{1,0:T(8,128)(2,1)}, bf16[192,1280]{1,0:T(8,128)(2,1)S(1)}, u32[]{:S(2)}, u32[]{:S(2)}) %collective-permute-start.16) | collective-permute-done | bytes 491552 | tf_op jit(solution)/shard_map/ppermute | solution.py:61
  110.6 4.3 %collective-permute-done.17.dep_2 = bf16[192,1280]{1,0:T(8,128)(2,1)S(1)} collective-permute-done((bf16[192,1280]{1,0:T(8,128)(2,1)}, bf16[192,1280]{1,0:T(8,128)(2,1)S(1)}, u32[]{:S(2)}, u32[]{:S(2)}) %collective-permute-start.17) | collective-permute-done | bytes 491552 | tf_op jit(solution)/shard_map/ppermute | solution.py:61
  117.1 3.2 %shard_map.90 = (bf16[128,2048]{1,0:T(8,128)(2,1)}, bf16[1,128]{1,0:T(2,128)(2,1)}) custom-call(bf16[4,128,2048]{2,1,0:T(8,128)(2,1)} %copy-done.2, bf16[128,2048]{1,0:T(8,128)(2,1)} %weight_ref.3, bf16[1,128]{1,0:T(2,128)(2,1)} %bitcast.11, bf16[192,1280]{1,0:T(8,128)(2,1)} %copy-done, bf16[192,1280]{1,0:T(8,128)(2,1)} %copy-done.1), custom_call_target="tpu_custom_call" | custom-call | bytes 6029312 | tf_op jit(solution)/shard_map/pallas_call | solution.py:35
  120.3 19.2 %conditional.1 = (bf16[128,2048]{1,0:T(8,128)(2,1)}, bf16[1,128]{1,0:T(2,128)(2,1)}, bf16[192,2048]{1,0:T(8,128)(2,1)}, bf16[192,2048]{1,0:T(8,128)(2,1)}) conditional(s32[]{:T(128)} %clamp.3, (bf16[128,2048]{1,0:T(8,128)(2,1)}, bf16[1,128]{1,0:T(2,128)(2,1)}, s32[1]{0:T(128)}, bf16[192,2048]{1,0:T(8,128)(2,1)}, ...), branch_computations={%region_0.1_spmd, %region_1.2_spmd, %region_2.3_spmd, %region_3.4_... | conditional | bytes 8127600 | solution.py:387
  122.2 5.3 %collective-permute-start.1 = (bf16[1,128]{1,0:T(2,128)(2,1)}, bf16[1,128]{1,0:T(2,128)(2,1)}, u32[]{:S(2)}, u32[]{:S(2)}) collective-permute-start(bf16[1,128]{1,0:T(2,128)(2,1)} %get-tuple-element.89), channel_id=1, source_target_pairs={{0,16},{16,32},{32,48},{48,64},{64,80},{80,96},{96,112},{112,128},... | collective-permute-start | bytes 776 | tf_op jit(solution)/shard_map/cond/branch_0_fun/ppermute | solution.py:61
  127.5 4.5 %branch_0_fun.1 = (bf16[192,2048]{1,0:T(8,128)(2,1)}, bf16[192,2048]{1,0:T(8,128)(2,1)}) custom-call(s32[1]{0:T(128)} %get-tuple-element.90.me_ref, bf16[192,2048]{1,0:T(8,128)(2,1)} %get-tuple-element.91.tok_ref, f32[192,128]{1,0:T(8,128)} %get-tuple-element.92.rstd_ref, f32[192,2048]{1,0:T(8,128)} %get-tuple-element.93.p0, ...), custom_call_target="tpu_custom_call" | custom-call | bytes 6029312 | tf_op jit(solution)/shard_map/cond/branch_0_fun/pallas_call | solution.py:35
  132.0 7.4 %collective-permute-done.1 = bf16[1,128]{1,0:T(2,128)(2,1)} collective-permute-done((bf16[1,128]{1,0:T(2,128)(2,1)}, bf16[1,128]{1,0:T(2,128)(2,1)}, u32[]{:S(2)}, u32[]{:S(2)}) %collective-permute-start.1) | collective-permute-done | bytes 288 | tf_op jit(solution)/shard_map/cond/branch_0_fun/ppermute | solution.py:61
  (42 shorter events, 28.0 us)
Async XLA Ops:
  3.2 57.9 %all-to-all-start.1 = ((bf16[4,128,2048]{2,1,0:T(8,128)(2,1)}), bf16[4,128,2048]{2,1,0:T(8,128)(2,1)S(1)}, u32[]{:S(2)}, u32[]{:S(2)}) async-start(bf16[4,128,2048]{2,1,0:T(8,128)(2,1)} %shard_map.84.dep_ref), calls=%async_computation.1 | async-start | bytes 4194304 | tf_op jit(solution)/shard_map/all_to_all | solution.py:65
  13.0 16.3 %collective-permute-start.10 = (bf16[192,1280]{1,0:T(8,128)(2,1)}, bf16[192,1280]{1,0:T(8,128)(2,1)S(1)}, u32[]{:S(2)}, u32[]{:S(2)}) collective-permute-start(bf16[192,1280]{1,0:T(8,128)(2,1)} %get-tuple-element.171.sa), channel_id=1, source_target_pairs={{0,1},{1,2},{2,3},{3,0},{4,5},{5,6},{6,7},{7,4},{8,9},{9,10},{10,1... | collective-permute-start | bytes 1474568 | tf_op jit(solution)/shard_map/ppermute | solution.py:61
  15.4 17.5 %collective-permute-start.12 = (bf16[192,1280]{1,0:T(8,128)(2,1)}, bf16[192,1280]{1,0:T(8,128)(2,1)S(1)}, u32[]{:S(2)}, u32[]{:S(2)}) collective-permute-start(bf16[192,1280]{1,0:T(8,128)(2,1)} %get-tuple-element.172.sb), channel_id=1, source_target_pairs={{0,3},{1,0},{2,1},{3,2},{4,7},{5,4},{6,5},{7,6},{8,11},{9,8},{10,9... | collective-permute-start | bytes 1474568 | tf_op jit(solution)/shard_map/ppermute | solution.py:61
  18.8 23.0 %collective-permute-start.8 = (bf16[192,1536]{1,0:T(8,128)(2,1)}, bf16[192,1536]{1,0:T(8,128)(2,1)S(1)}, u32[]{:S(2)}, u32[]{:S(2)}) collective-permute-start(bf16[192,1536]{1,0:T(8,128)(2,1)} %get-tuple-element.169), channel_id=1, source_target_pairs={{0,1},{1,2},{2,3},{3,0},{4,5},{5,6},{6,7},{7,4},{8,9},{9,10},{10,1... | collective-permute-start | bytes 1769480 | tf_op jit(solution)/shard_map/ppermute | solution.py:61
  22.4 23.0 %collective-permute-start.9 = (bf16[192,1536]{1,0:T(8,128)(2,1)}, bf16[192,1536]{1,0:T(8,128)(2,1)S(1)}, u32[]{:S(2)}, u32[]{:S(2)}) collective-permute-start(bf16[192,1536]{1,0:T(8,128)(2,1)} %get-tuple-element.170), channel_id=1, source_target_pairs={{0,3},{1,0},{2,1},{3,2},{4,7},{5,4},{6,5},{7,6},{8,11},{9,8},{10,9... | collective-permute-start | bytes 1769480 | tf_op jit(solution)/shard_map/ppermute | solution.py:61
  29.2 24.7 %copy-start.10 = (bf16[192,1280]{1,0:T(8,128)(2,1)}, bf16[192,1280]{1,0:T(8,128)(2,1)S(1)}, u32[]{:S(2)}) copy-start(bf16[192,1280]{1,0:T(8,128)(2,1)S(1)} %collective-permute-done.10.la) | copy-start | bytes 1474564
  29.2 21.4 %collective-permute-start.11 = (bf16[192,1280]{1,0:T(8,128)(2,1)S(1)}, bf16[192,1280]{1,0:T(8,128)(2,1)S(1)}, u32[]{:S(2)}, u32[]{:S(2)}) collective-permute-start(bf16[192,1280]{1,0:T(8,128)(2,1)S(1)} %collective-permute-done.10.la), channel_id=1, source_target_pairs={{0,1},{1,2},{2,3},{3,0},{4,5},{5,6},{6,7},{7,4},{8,9},{9,10},{10,1... | collective-permute-start | bytes 1474568 | tf_op jit(solution)/shard_map/ppermute | solution.py:61
  32.8 21.1 %copy-start.11 = (bf16[192,1280]{1,0:T(8,128)(2,1)}, bf16[192,1280]{1,0:T(8,128)(2,1)S(1)}, u32[]{:S(2)}) copy-start(bf16[192,1280]{1,0:T(8,128)(2,1)S(1)} %collective-permute-done.12.rb) | copy-start | bytes 1474564
  32.8 21.1 %collective-permute-start.13 = (bf16[192,1280]{1,0:T(8,128)(2,1)S(1)}, bf16[192,1280]{1,0:T(8,128)(2,1)S(1)}, u32[]{:S(2)}, u32[]{:S(2)}) collective-permute-start(bf16[192,1280]{1,0:T(8,128)(2,1)S(1)} %collective-permute-done.12.rb), channel_id=1, source_target_pairs={{0,3},{1,0},{2,1},{3,2},{4,7},{5,4},{6,5},{7,6},{8,11},{9,8},{10,9... | collective-permute-start | bytes 1474568 | tf_op jit(solution)/shard_map/ppermute | solution.py:61
  41.9 12.1 %copy-start.6 = (bf16[192,1536]{1,0:T(8,128)(2,1)}, bf16[192,1536]{1,0:T(8,128)(2,1)S(1)}, u32[]{:S(2)}) copy-start(bf16[192,1536]{1,0:T(8,128)(2,1)S(1)} %collective-permute-done.8.lt) | copy-start | bytes 1769476
  45.5 8.5 %copy-start.7 = (bf16[192,1536]{1,0:T(8,128)(2,1)}, bf16[192,1536]{1,0:T(8,128)(2,1)S(1)}, u32[]{:S(2)}) copy-start(bf16[192,1536]{1,0:T(8,128)(2,1)S(1)} %collective-permute-done.9.rt) | copy-start | bytes 1769476
  50.6 3.4 %copy-start.4 = (bf16[192,1280]{1,0:T(8,128)(2,1)}, bf16[192,1280]{1,0:T(8,128)(2,1)S(1)}, u32[]{:S(2)}) copy-start(bf16[192,1280]{1,0:T(8,128)(2,1)S(1)} %collective-permute-done.11.fa) | copy-start | bytes 1474564
  61.2 1.3 copy-start.3
  62.5 52.5 %all-to-all-start = ((bf16[4,128,2048]{2,1,0:T(8,128)(2,1)}), bf16[4,128,2048]{2,1,0:T(8,128)(2,1)S(1)}, u32[]{:S(2)}, u32[]{:S(2)}) async-start(bf16[4,128,2048]{2,1,0:T(8,128)(2,1)} %shard_map.86.dep), calls=%async_computation | async-start | bytes 4194304 | tf_op jit(solution)/shard_map/all_to_all | solution.py:65
  73.7 18.0 %collective-permute-start.14 = (bf16[192,1280]{1,0:T(8,128)(2,1)}, bf16[192,1280]{1,0:T(8,128)(2,1)S(1)}, u32[]{:S(2)}, u32[]{:S(2)}) collective-permute-start(bf16[192,1280]{1,0:T(8,128)(2,1)} %get-tuple-element.173.dep), channel_id=1, source_target_pairs={{0,1},{1,2},{2,3},{3,0},{4,5},{5,6},{6,7},{7,4},{8,9},{9,10},{10,1... | collective-permute-start | bytes 1474568 | tf_op jit(solution)/shard_map/ppermute | solution.py:61
  75.9 15.8 %collective-permute-start.15 = (bf16[192,1280]{1,0:T(8,128)(2,1)}, bf16[192,1280]{1,0:T(8,128)(2,1)S(1)}, u32[]{:S(2)}, u32[]{:S(2)}) collective-permute-start(bf16[192,1280]{1,0:T(8,128)(2,1)} %get-tuple-element.176), channel_id=1, source_target_pairs={{0,3},{1,0},{2,1},{3,2},{4,7},{5,4},{6,5},{7,6},{8,11},{9,8},{10,9... | collective-permute-start | bytes 1474568 | tf_op jit(solution)/shard_map/ppermute | solution.py:61
  85.8 34.5 %collective-permute-start.18 = (bf16[192,1536]{1,0:T(8,128)(2,1)}, bf16[192,1536]{1,0:T(8,128)(2,1)}, u32[]{:S(2)}, u32[]{:S(2)}) collective-permute-start(bf16[192,1536]{1,0:T(8,128)(2,1)} %get-tuple-element.184), channel_id=1, source_target_pairs={{0,1},{1,2},{2,3},{3,0},{4,5},{5,6},{6,7},{7,4},{8,9},{9,10},{10,1... | collective-permute-start | bytes 1769480 | tf_op jit(solution)/shard_map/ppermute | solution.py:61
  89.2 31.1 %collective-permute-start.19 = (bf16[192,1536]{1,0:T(8,128)(2,1)}, bf16[192,1536]{1,0:T(8,128)(2,1)}, u32[]{:S(2)}, u32[]{:S(2)}) collective-permute-start(bf16[192,1536]{1,0:T(8,128)(2,1)} %get-tuple-element.185), channel_id=1, source_target_pairs={{0,3},{1,0},{2,1},{3,2},{4,7},{5,4},{6,5},{7,6},{8,11},{9,8},{10,9... | collective-permute-start | bytes 1769480 | tf_op jit(solution)/shard_map/ppermute | solution.py:61
  95.4 15.3 %collective-permute-start.16 = (bf16[192,1280]{1,0:T(8,128)(2,1)}, bf16[192,1280]{1,0:T(8,128)(2,1)S(1)}, u32[]{:S(2)}, u32[]{:S(2)}) collective-permute-start(bf16[192,1280]{1,0:T(8,128)(2,1)} %get-tuple-element.177), channel_id=1, source_target_pairs={{0,1},{1,2},{2,3},{3,0},{4,5},{5,6},{6,7},{7,4},{8,9},{9,10},{10,1... | collective-permute-start | bytes 1474568 | tf_op jit(solution)/shard_map/ppermute | solution.py:61
  100.0 15.0 %collective-permute-start.17 = (bf16[192,1280]{1,0:T(8,128)(2,1)}, bf16[192,1280]{1,0:T(8,128)(2,1)S(1)}, u32[]{:S(2)}, u32[]{:S(2)}) collective-permute-start(bf16[192,1280]{1,0:T(8,128)(2,1)} %get-tuple-element.178), channel_id=1, source_target_pairs={{0,3},{1,0},{2,1},{3,2},{4,7},{5,4},{6,5},{7,6},{8,11},{9,8},{10,9... | collective-permute-start | bytes 1474568 | tf_op jit(solution)/shard_map/ppermute | solution.py:61
  110.6 4.4 %copy-start = (bf16[192,1280]{1,0:T(8,128)(2,1)}, bf16[192,1280]{1,0:T(8,128)(2,1)S(1)}, u32[]{:S(2)}) copy-start(bf16[192,1280]{1,0:T(8,128)(2,1)S(1)} %collective-permute-done.16.dep_1) | copy-start | bytes 1474564
  115.8 1.3 copy-start.2
  120.3 19.2 %collective-permute-start = (bf16[128,2048]{1,0:T(8,128)(2,1)}, bf16[128,2048]{1,0:T(8,128)(2,1)}, u32[]{:S(2)}, u32[]{:S(2)}) collective-permute-start(bf16[128,2048]{1,0:T(8,128)(2,1)} %get-tuple-element.88), channel_id=1, source_target_pairs={{0,16},{16,32},{32,48},{48,64},{64,80},{80,96},{96,112},{112,128},... | collective-permute-start | bytes 1572872 | tf_op jit(solution)/shard_map/cond/branch_0_fun/ppermute | solution.py:61
  122.2 17.2 %collective-permute-start.1 = (bf16[1,128]{1,0:T(2,128)(2,1)}, bf16[1,128]{1,0:T(2,128)(2,1)}, u32[]{:S(2)}, u32[]{:S(2)}) collective-permute-start(bf16[1,128]{1,0:T(2,128)(2,1)} %get-tuple-element.89), channel_id=1, source_target_pairs={{0,16},{16,32},{32,48},{48,64},{64,80},{80,96},{96,112},{112,128},... | collective-permute-start | bytes 776 | tf_op jit(solution)/shard_map/cond/branch_0_fun/ppermute | solution.py:61
  (4 other events, 3.3 us)

commit v3 on v2

v3 whole, which is shorter than its diff:
```python
import functools
import math

import jax
import jax.numpy as jnp
from jax import lax
from jax.experimental import pallas as pl
from jax.experimental.pallas import tpu as pltpu
from jax.sharding import Mesh
from jax.sharding import PartitionSpec as P

eps = 1e-05
step_rate = 0.75
gain_rate = 0.004
F32 = jnp.float32
BF16 = jnp.bfloat16
VMEM_LIMIT = 32 * 1024 * 1024
ANY = pl.BlockSpec(memory_space=pl.ANY)
DEP = pl.BlockSpec(memory_space=pl.ANY)
BLOCK, AUTO = "block", "auto"
HERE = pl.BlockSpec(memory_space=pltpu.VMEM)
SCALAR = pl.BlockSpec(memory_space=pltpu.SMEM)


def array(shape, dtype=BF16):
    return jax.ShapeDtypeStruct(shape, dtype)


def in_hbm(shape, dtype=BF16):
    return pltpu.HBM(shape, dtype)


def call(kernel, ins, outs, scratch=(), flops=0, moved=0, passed={}):
    values = [
        pltpu.with_memory_space_constraint(v, pltpu.HBM) if spec is ANY or spec is BLOCK else v
        for v, spec in ins
    ]
    return pl.pallas_call(
        kernel,
        grid=(1,),
        out_shape=list(outs),
        in_specs=[whole(v.shape) if spec in (BLOCK, AUTO) else spec for v, spec in ins],
        out_specs=[
            DEP if i in passed.values() else HERE if isinstance(shape, jax.ShapeDtypeStruct) else whole(shape.shape)
            for i, shape in enumerate(outs)
        ],
        input_output_aliases=passed,
        scratch_shapes=list(scratch),
        compiler_params=pltpu.CompilerParams(vmem_limit_bytes=VMEM_LIMIT),
        cost_estimate=pl.CostEstimate(flops=flops, bytes_accessed=moved, transcendentals=0),
    )(*values)


def whole(shape):
    return pl.BlockSpec(shape, lambda s: (0,) * len(shape))


def fetch(pairs, sems):
    copies = [pltpu.make_async_copy(src, dst, sems.at[i]) for i, (src, dst) in enumerate(pairs)]
    for copy in copies:
        copy.start()
    return copies


def shifted(value, axis, steps):
    count = lax.axis_size(axis)
    pairs = [(source, (source + steps) % count) for source in range(count)]
    return lax.ppermute(value, axis, pairs)


def exchange(blocks, axis):
    return lax.all_to_all(blocks, axis, split_axis=0, concat_axis=0, tiled=True)


def column_of(row):
    n = row.shape[1]
    down = lax.broadcasted_iota(jnp.int32, (n, n), 0)
    along = lax.broadcasted_iota(jnp.int32, (n, n), 1)
    return jnp.sum(jnp.where(down == along, row, 0.0), axis=1, keepdims=True)


def row_of(column):
    n = column.shape[0]
    down = lax.broadcasted_iota(jnp.int32, (n, n), 0)
    along = lax.broadcasted_iota(jnp.int32, (n, n), 1)
    return jnp.sum(jnp.where(down == along, column, 0.0), axis=0, keepdims=True)


def weight_kernel(gain_ref, weight_ref, out_ref):
    scaled = (weight_ref[...].astype(F32) * column_of(gain_ref[...].astype(F32))).astype(BF16)
    for i in range(out_ref.shape[0]):
        out_ref[i] = scaled


def token_kernel(
    n_x, me_ref, tok, up, dep, own_ref, sa_ref, sb_ref, ta_ref, tb_ref, rstd_ref, vt, vu, sems
):
    fetched = fetch([(tok, vt), (up, vu)], sems)
    me = me_ref[0]
    width, part = vt.shape[1], own_ref.shape[1]
    rows = part // (width // part)
    half, quarter = width // 2, part // 2
    fetched[0].wait()
    for d in range(n_x):
        slot = lax.rem(me + d, n_x) * rows
        for k in range(part // rows):
            block = vt[:, pl.ds(pl.multiple_of(slot + k * n_x * rows, rows), rows)]
            at = k * rows
            if d == 0:
                own_ref[:, at : at + rows] = block
            elif d == 1:
                ta_ref[:, half + at : half + at + rows] = block
            elif d == 3:
                tb_ref[:, half + at : half + at + rows] = block
            elif at < quarter:
                sa_ref[:, half + at : half + at + rows] = block
            else:
                sb_ref[:, half + at - quarter : half + at - quarter + rows] = block
    x = vt[...].astype(F32)
    rstd = lax.rsqrt(jnp.mean(x * x, axis=1, keepdims=True) + eps)
    rstd_ref[...] = jnp.broadcast_to(rstd, rstd_ref.shape)
    fetched[1].wait()
    up_a = (vu[:, :half].astype(F32) * rstd).astype(BF16)
    up_b = (vu[:, half:].astype(F32) * rstd).astype(BF16)
    sa_ref[:, :half] = up_a
    tb_ref[:, :half] = up_a
    sb_ref[:, :half] = up_b
    ta_ref[:, :half] = up_b


def grad_kernel(xo, lt, rt, sa, la, sb, rb, out, vx, vlt, vrt, vsa, vla, vsb, vrb, turned, sems):
    half = vsa.shape[1]
    tile = 256
    copies = fetch(
        [
            (xo, vx),
            (lt, vlt),
            (rt, vrt),
            (sa.at[:, :half], vsa),
            (la.at[:, :half], vla),
            (sb.at[:, :half], vsb),
            (rb.at[:, :half], vrb),
        ],
        sems,
    )
    for copy in copies[:3]:
        copy.wait()
    turned[...] = jnp.concatenate([vx[...], vlt[:, half:], vrt[:, half:]], axis=0).T
    for h, refs in enumerate(((vsa, vla, vrt), (vsb, vlt, vrb))):
        for copy in copies[3 + 2 * h : 5 + 2 * h]:
            copy.wait()

        @pl.loop(0, half // tile)
        def _(j):
            cols = pl.ds(pl.multiple_of(j * tile, tile), tile)
            block = jnp.concatenate([r[:, cols] for r in refs], axis=0)
            to = pl.ds(pl.multiple_of(h * half + j * tile, tile), tile)
            out[:, to] = jnp.dot(turned[...], block, preferred_element_type=F32)


def grad_far_kernel(scale, near, fa, fb, out, turned):
    half = near.shape[1] // 2
    rows = out.shape[1]
    tile = 256
    turned[...] = jnp.concatenate([fa[:, half:], fb[:, half:]], axis=1).T
    for h, ref in enumerate((fa, fb)):

        @pl.loop(0, half // tile)
        def _(j):
            cols = pl.ds(pl.multiple_of(j * tile, tile), tile)
            to = pl.ds(pl.multiple_of(h * half + j * tile, tile), tile)
            total = near[:, to] + jnp.dot(turned[...], ref[:, cols], preferred_element_type=F32)
            total = (total * scale).astype(BF16)
            for k in range(out.shape[0]):
                out[k, :, to] = total[k * rows : (k + 1) * rows]


def times_turned(left, right):
    return lax.dot_general(left, right, (((1,), (1,)), ((), ())), preferred_element_type=F32)


def far_kernel(scale, fa, fb, w, dep, out_a, out_b, vw, sems):
    part, width = w.shape
    half, quarter = width // 2, part // 2
    pieces = [(w.at[:, i * half : (i + 1) * half], vw.at[:, i * half : (i + 1) * half]) for i in range(2)]
    copies = fetch(pieces, sems)
    x = jnp.concatenate([fa[:, half:], fb[:, half:]], axis=1)
    g = 0.0
    for h, (u, out) in enumerate(((fa, out_a), (fb, out_b))):
        copies[h].wait()
        block = vw[:, h * half : (h + 1) * half]
        out[:, :half] = (jnp.dot(x, block, preferred_element_type=F32) * scale).astype(BF16)
        g = g + times_turned(u[:, :half], block)
    g = (g * scale).astype(BF16)
    out_a[:, half:] = g[:, :quarter]
    out_b[:, half:] = g[:, quarter:]


def near_kernel(
    scale, xo, lt, rt, sa, la, sb, rb, w, dep, p0, g0, tr, tl, pr, pl_, vx, vlt, vrt, vsa, vla, vsb, vrb, vw, sems
):
    part = w.shape[0]
    count, half = vsa.shape
    tile = half // 2
    copies = fetch(
        [
            (xo, vx),
            (lt, vlt),
            (rt, vrt),
            (sa.at[:, :half], vsa),
            (la.at[:, :half], vla),
            (sb.at[:, :half], vsb),
            (rb.at[:, :half], vrb),
            (w.at[:, :half], vw.at[:, :half]),
            (w.at[:, half:], vw.at[:, half:]),
        ],
        sems,
    )
    for copy in copies[:3]:
        copy.wait()
    x = jnp.concatenate([vx[...], vlt[:, half:], vrt[:, half:]], axis=0)
    for h in range(2):
        copies[7 + h].wait()
        for t in range(2):
            at = h * half + t * tile
            cols = slice(t * tile, (t + 1) * tile)
            p = jnp.dot(x, vw[:, at : at + tile], preferred_element_type=F32) * scale
            p0[:, at : at + tile] = p[:count]
            if h == 0:
                tl[:, cols] = p[count : 2 * count].astype(BF16)
                pr[:, cols] = p[2 * count :]
            else:
                tr[:, cols] = p[2 * count :].astype(BF16)
                pl_[:, cols] = p[count : 2 * count]
    for copy in copies[3:7]:
        copy.wait()
    up_a = jnp.concatenate([vsa[...], vla[...], vrt[:, :half]], axis=0)
    up_b = jnp.concatenate([vsb[...], vlt[:, :half], vrb[...]], axis=0)
    for k in range(0, part, 256):
        g = times_turned(up_a, vw[k : k + 256, :half]) + times_turned(up_b, vw[k : k + 256, half:])
        g = (g * scale).astype(BF16)
        g0[:, k : k + 256] = g[:count]
        tl[:, half + k : half + k + 256] = g[count : 2 * count]
        tr[:, half + k : half + k + 256] = g[2 * count :]


def pass_kernel(pr, pl_, in_a, in_b, dr, dl):
    half = pr.shape[1]
    dr[:, :half] = (pr[...] + in_a[:, :half].astype(F32)).astype(BF16)
    dr[:, half:] = in_a[:, half:]
    dl[:, :half] = (pl_[...] + in_b[:, :half].astype(F32)).astype(BF16)
    dl[:, half:] = in_b[:, half:]


def result_kernel(n_x, me_ref, tok_ref, rstd_ref, p0, g0, lt, ld, rt, rd, out_p, out_x, back):
    me = me_ref[0]
    width, part = tok_ref.shape[1], g0.shape[1]
    rows = part // (width // part)
    half, quarter = width // 2, part // 2
    rstd = rstd_ref[:, :1]
    for h, (l, r) in enumerate(((ld, rt), (lt, rd))):
        cols = slice(h * half, (h + 1) * half)
        total = p0[:, cols] + l[:, :half].astype(F32) + r[:, :half].astype(F32)
        out_p[:, cols] = (total * rstd).astype(BF16)
    for d in range(n_x):
        slot = lax.rem(me + d, n_x) * rows
        for k in range(part // rows):
            at = k * rows
            if d == 0:
                block = g0[:, at : at + rows]
            elif d == 1:
                block = rt[:, half + at : half + at + rows]
            elif d == 3:
                block = lt[:, half + at : half + at + rows]
            elif at < quarter:
                block = ld[:, half + at : half + at + rows]
            else:
                block = rd[:, half + at - quarter : half + at - quarter + rows]
            back[:, pl.ds(pl.multiple_of(slot + k * n_x * rows, rows), rows)] = block.astype(F32)
    g = back[...]
    xhat = tok_ref[...].astype(F32) * rstd
    mean = jnp.mean(g * xhat, axis=1, keepdims=True)
    out_x[...] = (g - xhat * mean).astype(BF16)


def step_kernel(parts_ref, weight_ref, gain_ref, dep_1, dep_2, out_ref):
    width = weight_ref.shape[1]
    column = column_of(gain_ref[...].astype(F32))
    grad = jnp.sum(parts_ref[...].astype(F32), axis=0)
    w = weight_ref[...].astype(F32)
    slope = jnp.sum(grad * w, axis=1, keepdims=True)
    out_ref[:, :width] = (w - step_rate * (column * grad)).astype(BF16)
    stepped = (column - gain_rate * slope).astype(BF16)
    out_ref[:, width:] = jnp.broadcast_to(stepped, (stepped.shape[0], out_ref.shape[1] - width))


def mean_kernel(mine, peer, out_w_ref, out_g_ref):
    width = out_w_ref.shape[1]
    out_w_ref[...] = (0.5 * (mine[:, :width].astype(F32) + peer[:, :width].astype(F32))).astype(BF16)
    column = 0.5 * (mine[:, width : width + 1].astype(F32) + peer[:, width : width + 1].astype(F32))
    out_g_ref[...] = row_of(column).astype(BF16)


def on_device(tokens, weight, gain, upstream, step):
    n_x, n_y = lax.axis_size("x"), lax.axis_size("yh")
    rows, width_out = weight.shape
    count, width_in = tokens.shape
    scale = 1.0 / math.sqrt(width_in)
    half = width_out // 2
    part = n_y * rows
    me = jnp.stack([lax.axis_index("x"), lax.axis_index("yh")]).astype(jnp.int32)
    gain_row = gain.reshape(1, rows)
    flops = 2 * n_x * count * part * width_out
    moved = 2 * (n_x * count * (part + width_out) + part * width_out)
    quarter = part // 2
    vmem = lambda *shape: pltpu.VMEM(shape, BF16)
    sems = lambda n: pltpu.SemaphoreType.DMA((n,))
    short, long = (count, half + quarter), (count, half + part)

    (copies,) = call(
        weight_kernel, [(gain_row, BLOCK), (weight, BLOCK)], [in_hbm((n_y, rows, width_out))]
    )
    full_weight = exchange(copies, "yh").reshape(part, width_out)

    x_own, sa, sb, ta, tb, rstd = call(
        functools.partial(token_kernel, n_x),
        [(me, SCALAR), (tokens, ANY), (upstream, ANY), (copies, DEP)],
        [
            in_hbm((count, part)),
            in_hbm(short),
            in_hbm(short),
            array(long),
            array(long),
            in_hbm((count, 128), F32),
        ],
        [vmem(count, width_in), vmem(count, width_out), sems(2)],
    )
    la, rb = shifted(sa, "x", 1), shifted(sb, "x", -1)
    lt, rt = shifted(ta, "x", 1), shifted(tb, "x", -1)
    fa, fb = shifted(la, "x", 1), shifted(rb, "x", -1)

    near = [(v, ANY) for v in (x_own, lt, rt, sa, la, sb, rb)]
    near_scratch = [vmem(count, part)] + [vmem(*long)] * 2 + [vmem(count, half)] * 4
    (near_w,) = call(
        grad_kernel,
        near,
        [array((part, width_out), F32)],
        near_scratch + [vmem(part, 3 * count), sems(7)],
        flops * 3 // 4,
        moved,
    )
    (part_w,) = call(
        functools.partial(grad_far_kernel, scale),
        [(near_w, HERE), (fa, HERE), (fb, HERE)],
        [array((n_y, rows, width_out))],
        [vmem(part, count)],
        flops // 4,
        moved,
    )

    pieces_w = exchange(part_w, "yh")
    out_a, out_b = call(
        functools.partial(far_kernel, scale),
        [(fa, HERE), (fb, HERE), (full_weight, DEP), (part_w, DEP)],
        [array(short), array(short)],
        [vmem(part, width_out), sems(2)],
        flops // 2,
        moved // 2,
    )
    in_a, in_b = shifted(out_a, "x", 1), shifted(out_b, "x", -1)
    p0, g0, tr, tl, pr, pl_ = call(
        functools.partial(near_kernel, scale),
        near + [(full_weight, DEP), (out_a, DEP)],
        [in_hbm((count, width_out), F32), in_hbm((count, part)), array(long), array(long)]
        + [array((count, half), F32)] * 2,
        near_scratch + [vmem(part, width_out), sems(9)],
        2 * flops,
        2 * moved,
    )
    got_lt, got_rt = shifted(tr, "x", 1), shifted(tl, "x", -1)
    dr, dl = call(
        pass_kernel,
        [(pr, HERE), (pl_, HERE), (in_a, HERE), (in_b, HERE)],
        [array(short), array(short)],
        moved=moved,
    )
    got_ld, got_rd = shifted(dr, "x", 1), shifted(dl, "x", -1)

    (stepped,) = call(
        step_kernel,
        [(v, HERE) for v in (pieces_w, weight, gain_row)] + [(got_ld, DEP), (got_rd, DEP)],
        [array((rows, width_out + 128))],
        moved=moved,
    )

    def gossip(distance):
        def branch(stepped, rest):
            peer = shifted(stepped, "rep", distance)
            results = call(
                functools.partial(result_kernel, n_x),
                [(rest[0], SCALAR)] + [(v, BLOCK) for v in rest[1:]],
                [in_hbm((count, width_out)), in_hbm((count, width_in))],
                [pltpu.VMEM((count, width_in), F32)],
                moved=moved,
            )
            means = call(
                mean_kernel,
                [(stepped, HERE), (peer, HERE)],
                [in_hbm((rows, width_out)), in_hbm((1, rows))],
            )
            return *results, *means

        return branch

    projected, input_gradient, new_weight, new_gain = lax.switch(
        step[0] % 4,
        [gossip(distance) for distance in (1, 2, 4, 8)],
        stepped,
        (me, tokens, rstd, p0, g0, got_lt, got_ld, got_rt, got_rd),
    )
    return projected, input_gradient, new_weight, new_gain.reshape(rows)


def solution(mesh):
    n_rep, n_fsdp = mesh.devices.shape
    n_x = 4
    split = Mesh(mesh.devices.reshape(n_rep, n_fsdp // n_x, n_x), ("rep", "yh", "x"))
    every = ("rep", "yh", "x")
    placed = (P(every, None), P(every, None), P(every), P(every, None), P())
    return jax.shard_map(
        on_device,
        mesh=split,
        in_specs=placed,
        out_specs=(P(every, None), P(every, None), P(every, None), P(every)),
        check_vma=False,
    )
```

time: 142 us -> 133 us (0.937)
  the two profiles are of different devices: /device:TPU:30 before, /device:TPU:24 now
where the time goes in v3:
time: 133 us; the launch traced here: 132 us
  starting transfers between devices  56.6 us (43%)
  waiting for transfers between devices  43 us (32%)
  Pallas kernels  29.8 us (22%)
  between operations  1.5 us (1%)
    ppermute x13, starting transfers between devices, shifted(): return lax.ppermute(value, axis, pairs)  44.4 us
    ppermute x13, waiting for transfers between devices, shifted(): return lax.ppermute(value, axis, pairs)  37.5 us
    pallas_call x10, Pallas kernels, call(): pl.pallas_call(kernel, grid=(1,), out_shape=list(outs), in_specs=[whole(v...  29.8 us
    all_to_all x2, starting transfers between devices, exchange(): return lax.all_to_all(blocks, axis, split_axis=0, concat_axis=0, tiled=True)  12.3 us
    all_to_all x2, waiting for transfers between devices, exchange(): return lax.all_to_all(blocks, axis, split_axis=0, concat_axis=0, tiled=True)  5.46 us
  transfers between devices with their start and end apart: 15, of which 10 were waited for; matrix products, arithmetic and copies ran while one was open for 0% of the time, Pallas kernels for 20%

profile of v3, /device:TPU:24, one launch (start us, length us, event | category | flops | bytes accessed | tf_op | source)
XLA Modules:
  0.0 131.9 jit_solution(15220052416224803236)
XLA Ops:
  0.6 2.7 %shard_map.84.dep = bf16[4,128,2048]{2,1,0:T(8,128)(2,1)} custom-call(bf16[1,128]{1,0:T(2,128)(2,1)} %bitcast.9, bf16[128,2048]{1,0:T(8,128)(2,1)} %weight_ref.3), custom_call_target="tpu_custom_call" | custom-call | tf_op jit(solution)/shard_map/pallas_call | solution.py:38
  3.3 6.7 %all-to-all-start = ((bf16[4,128,2048]{2,1,0:T(8,128)(2,1)}), bf16[4,128,2048]{2,1,0:T(8,128)(2,1)}, u32[]{:S(2)}, u32[]{:S(2)}) async-start(bf16[4,128,2048]{2,1,0:T(8,128)(2,1)} %shard_map.84.dep), calls=%async_computation | async-start | bytes 4194304 | tf_op jit(solution)/shard_map/all_to_all | solution.py:72
  10.0 3.1 %shard_map.85 = (bf16[192,512]{1,0:T(8,128)(2,1)}, bf16[192,1280]{1,0:T(8,128)(2,1)}, bf16[192,1280]{1,0:T(8,128)(2,1)}, bf16[192,1536]{1,0:T(8,128)(2,1)S(1)}, ...) custom-call(s32[2]{0:T(128)S(1)} %pad_add_fusion.me_ref, bf16[192,2048]{1,0:T(8,128)(2,1)} %tok.1, ...), custom_call_target="tpu_custom_call" | custom-call | tf_op jit(solution)/shard_map/pallas_call | solution.py:38
  13.2 3.4 %collective-permute-start.6 = (bf16[192,1280]{1,0:T(8,128)(2,1)}, bf16[192,1280]{1,0:T(8,128)(2,1)S(1)}, u32[]{:S(2)}, u32[]{:S(2)}) collective-permute-start(bf16[192,1280]{1,0:T(8,128)(2,1)} %get-tuple-element.164.sa), channel_id=1, source_target_pairs={{0,1},{1,2},{2,3},{3,0},{4,5},{5,6},{6,7},{7,4},{8,9},{9,10},{10,1... | collective-permute-start | bytes 1474568 | tf_op jit(solution)/shard_map/ppermute | solution.py:68
  16.6 3.7 %collective-permute-start.7 = (bf16[192,1280]{1,0:T(8,128)(2,1)}, bf16[192,1280]{1,0:T(8,128)(2,1)S(1)}, u32[]{:S(2)}, u32[]{:S(2)}) collective-permute-start(bf16[192,1280]{1,0:T(8,128)(2,1)} %get-tuple-element.165.sb), channel_id=1, source_target_pairs={{0,3},{1,0},{2,1},{3,2},{4,7},{5,4},{6,5},{7,6},{8,11},{9,8},{10,9... | collective-permute-start | bytes 1474568 | tf_op jit(solution)/shard_map/ppermute | solution.py:68
  22.4 4.9 %collective-permute-start.5 = (bf16[192,1536]{1,0:T(8,128)(2,1)S(1)}, bf16[192,1536]{1,0:T(8,128)(2,1)S(1)}, u32[]{:S(2)}, u32[]{:S(2)}) collective-permute-start(bf16[192,1536]{1,0:T(8,128)(2,1)S(1)} %get-tuple-element.163), channel_id=1, source_target_pairs={{0,3},{1,0},{2,1},{3,2},{4,7},{5,4},{6,5},{7,6},{8,11},{9,8},{10,9... | collective-permute-start | bytes 1769480 | tf_op jit(solution)/shard_map/ppermute | solution.py:68
  27.3 3.3 %collective-permute-done.6.la = bf16[192,1280]{1,0:T(8,128)(2,1)S(1)} collective-permute-done((bf16[192,1280]{1,0:T(8,128)(2,1)}, bf16[192,1280]{1,0:T(8,128)(2,1)S(1)}, u32[]{:S(2)}, u32[]{:S(2)}) %collective-permute-start.6) | collective-permute-done | bytes 491552 | tf_op jit(solution)/shard_map/ppermute | solution.py:68
  32.8 4.9 %collective-permute-start.9 = (bf16[192,1280]{1,0:T(8,128)(2,1)S(1)}, bf16[192,1280]{1,0:T(8,128)(2,1)S(1)}, u32[]{:S(2)}, u32[]{:S(2)}) collective-permute-start(bf16[192,1280]{1,0:T(8,128)(2,1)S(1)} %collective-permute-done.7.rb), channel_id=1, source_target_pairs={{0,3},{1,0},{2,1},{3,2},{4,7},{5,4},{6,5},{7,6},{8,11},{9,8},{10,9... | collective-permute-start | bytes 1474568 | tf_op jit(solution)/shard_map/ppermute | solution.py:68
  37.7 5.6 %collective-permute-done.4.lt = bf16[192,1536]{1,0:T(8,128)(2,1)S(1)} collective-permute-done((bf16[192,1536]{1,0:T(8,128)(2,1)S(1)}, bf16[192,1536]{1,0:T(8,128)(2,1)S(1)}, u32[]{:S(2)}, u32[]{:S(2)}) %collective-permute-start.4) | collective-permute-done | bytes 589856 | tf_op jit(solution)/shard_map/ppermute | solution.py:68
  46.3 4.6 %shard_map.86.near = f32[512,2048]{1,0:T(8,128)S(1)} custom-call(bf16[192,512]{1,0:T(8,128)(2,1)} %get-tuple-element.161.xo, bf16[192,1536]{1,0:T(8,128)(2,1)} %copy-done.3, bf16[192,1536]{1,0:T(8,128)(2,1)} %copy-done.4, bf16[192,1280]{1,0:T(8,128)(2,1)} %get-tuple-element.164.sa, bf16[192,1280]{1,0:T(8,128)(2,1)} %copy-done.5, ...), custom_call_target="tpu_custom_call" | custom-call | flops 1207959552 | bytes 6029312 | tf_op jit(solution)/shard_map/pallas_call | solution.py:38
  54.0 3.3 %shard_map.87.dep = bf16[4,128,2048]{2,1,0:T(8,128)(2,1)} custom-call(f32[512,2048]{1,0:T(8,128)S(1)} %shard_map.86.near, bf16[192,1280]{1,0:T(8,128)(2,1)S(1)} %collective-permute-done.8.fa, bf16[192,1280]{1,0:T(8,128)(2,1)S(1)} %collective-permute-done.9.fb), custom_call_target="tpu_custom_call" | custom-call | flops 402653184 | bytes 6029312 | tf_op jit(solution)/shard_map/pallas_call | solution.py:38
  58.8 5.6 %all-to-all-start.1 = ((bf16[4,128,2048]{2,1,0:T(8,128)(2,1)}), bf16[4,128,2048]{2,1,0:T(8,128)(2,1)S(1)}, u32[]{:S(2)}, u32[]{:S(2)}) async-start(bf16[4,128,2048]{2,1,0:T(8,128)(2,1)} %shard_map.87.dep), calls=%async_computation.1 | async-start | bytes 4194304 | tf_op jit(solution)/shard_map/all_to_all | solution.py:72
  64.4 2.7 %shard_map.88 = (bf16[192,1280]{1,0:T(8,128)(2,1)S(1)}, bf16[192,1280]{1,0:T(8,128)(2,1)S(1)}) custom-call(bf16[192,1280]{1,0:T(8,128)(2,1)S(1)} %collective-permute-done.8.fa, bf16[192,1280]{1,0:T(8,128)(2,1)S(1)} %collective-permute-done.9.fb, bf16[512,2048]{1,0:T(8,128)(2,1)} %bitcast.4.w, bf16[4,128,2048]{2,1,0:T(8,128)(2,1)} %shard_map.87.dep), custom_call_target="tpu_custom_call" | custom-call | flops 805306368 | bytes 3014656 | tf_op jit(solution)/shard_map/pallas_call | solution.py:38
  67.1 3.4 %collective-permute-start.11 = (bf16[192,1280]{1,0:T(8,128)(2,1)S(1)}, bf16[192,1280]{1,0:T(8,128)(2,1)S(1)}, u32[]{:S(2)}, u32[]{:S(2)}) collective-permute-start(bf16[192,1280]{1,0:T(8,128)(2,1)S(1)} %get-tuple-element.166.dep), channel_id=1, source_target_pairs={{0,1},{1,2},{2,3},{3,0},{4,5},{5,6},{6,7},{7,4},{8,9},{9,10},{10,1... | collective-permute-start | bytes 1474568 | tf_op jit(solution)/shard_map/ppermute | solution.py:68
  70.5 3.7 %collective-permute-start.12 = (bf16[192,1280]{1,0:T(8,128)(2,1)S(1)}, bf16[192,1280]{1,0:T(8,128)(2,1)S(1)}, u32[]{:S(2)}, u32[]{:S(2)}) collective-permute-start(bf16[192,1280]{1,0:T(8,128)(2,1)S(1)} %get-tuple-element.172), channel_id=1, source_target_pairs={{0,3},{1,0},{2,1},{3,2},{4,7},{5,4},{6,5},{7,6},{8,11},{9,8},{10,9... | collective-permute-start | bytes 1474568 | tf_op jit(solution)/shard_map/ppermute | solution.py:68
  74.2 6.1 %shard_map.89 = (f32[192,2048]{1,0:T(8,128)}, bf16[192,512]{1,0:T(8,128)(2,1)}, bf16[192,1536]{1,0:T(8,128)(2,1)}, bf16[192,1536]{1,0:T(8,128)(2,1)S(1)}, f32[19...) custom-call(bf16[192,512]{1,0:T(8,128)(2,1)} %get-tuple-element.161.xo, bf16[192,1536]{1,0:T(8,128)(2,1)} %copy-done.3, ...), custom_call_target="tpu_custom_call" | custom-call | flops 3221225472 | bytes 12058624 | tf_op jit(solution)/shard_map/pallas_call | solution.py:38
  80.3 2.3 %collective-permute-start.10 = (bf16[192,1536]{1,0:T(8,128)(2,1)}, bf16[192,1536]{1,0:T(8,128)(2,1)}, u32[]{:S(2)}, u32[]{:S(2)}) collective-permute-start(bf16[192,1536]{1,0:T(8,128)(2,1)} %get-tuple-element.169), channel_id=1, source_target_pairs={{0,1},{1,2},{2,3},{3,0},{4,5},{5,6},{6,7},{7,4},{8,9},{9,10},{10,1... | collective-permute-start | bytes 1769480 | tf_op jit(solution)/shard_map/ppermute | solution.py:68
  82.6 4.9 %collective-permute-start.14 = (bf16[192,1536]{1,0:T(8,128)(2,1)S(1)}, bf16[192,1536]{1,0:T(8,128)(2,1)}, u32[]{:S(2)}, u32[]{:S(2)}) collective-permute-start(bf16[192,1536]{1,0:T(8,128)(2,1)S(1)} %get-tuple-element.174), channel_id=1, source_target_pairs={{0,3},{1,0},{2,1},{3,2},{4,7},{5,4},{6,5},{7,6},{8,11},{9,8},{10,9... | collective-permute-start | bytes 1769480 | tf_op jit(solution)/shard_map/ppermute | solution.py:68
  90.5 5.1 %collective-permute-start.15 = (bf16[192,1280]{1,0:T(8,128)(2,1)}, bf16[192,1280]{1,0:T(8,128)(2,1)}, u32[]{:S(2)}, u32[]{:S(2)}) collective-permute-start(bf16[192,1280]{1,0:T(8,128)(2,1)} %get-tuple-element.175), channel_id=1, source_target_pairs={{0,3},{1,0},{2,1},{3,2},{4,7},{5,4},{6,5},{7,6},{8,11},{9,8},{10,9... | collective-permute-start | bytes 1474568 | tf_op jit(solution)/shard_map/ppermute | solution.py:68
  96.3 10.4 %collective-permute-done.13.dep_1 = bf16[192,1280]{1,0:T(8,128)(2,1)} collective-permute-done((bf16[192,1280]{1,0:T(8,128)(2,1)}, bf16[192,1280]{1,0:T(8,128)(2,1)}, u32[]{:S(2)}, u32[]{:S(2)}) %collective-permute-start.13) | collective-permute-done | bytes 491552 | tf_op jit(solution)/shard_map/ppermute | solution.py:68
  107.7 3.9 %all-to-all-done.1.parts_ref = bf16[4,128,2048]{2,1,0:T(8,128)(2,1)S(1)} async-done(((bf16[4,128,2048]{2,1,0:T(8,128)(2,1)}), bf16[4,128,2048]{2,1,0:T(8,128)(2,1)S(1)}, u32[]{:S(2)}, u32[]{:S(2)}) %all-to-all-start.1) | async-done | bytes 2097184 | tf_op jit(solution)/shard_map/all_to_all | solution.py:72
  112.3 19.6 %conditional.1 = (bf16[192,2048]{1,0:T(8,128)(2,1)}, bf16[192,2048]{1,0:T(8,128)(2,1)}, bf16[128,2048]{1,0:T(8,128)(2,1)}, bf16[1,128]{1,0:T(2,128)(2,1)}) conditional(s32[]{:T(128)} %clamp.3, (s32[2]{0:T(128)S(1)}, bf16[192,2048]{1,0:T(8,128)(2,1)}, f32[192,128]{1,0:T(8,128)}, f32[192,2048]{1,0:T(8,128)}, ...), branch_computations={%region_0.1_spmd, %region_1.2_spmd, %region_2.3_spmd, %region_3.4_... | conditional | bytes 8257608 | solution.py:415
  114.2 4.5 %branch_0_fun.2 = (bf16[192,2048]{1,0:T(8,128)(2,1)}, bf16[192,2048]{1,0:T(8,128)(2,1)}) custom-call(s32[2]{0:T(128)S(1)} %get-tuple-element.80.me_ref, bf16[192,2048]{1,0:T(8,128)(2,1)} %get-tuple-element.81.tok_ref, f32[192,128]{1,0:T(8,128)} %get-tuple-element.82.rstd_ref, f32[192,2048]{1,0:T(8,128)} %get-tuple-element.83.p0, ...), custom_call_target="tpu_custom_call" | custom-call | bytes 6029312 | tf_op jit(solution)/shard_map/cond/branch_0_fun/pallas_call | solution.py:38
  118.7 12.0 %collective-permute-done.peer = bf16[128,2176]{1,0:T(8,128)(2,1)S(1)} collective-permute-done((bf16[128,2176]{1,0:T(8,128)(2,1)S(1)}, bf16[128,2176]{1,0:T(8,128)(2,1)S(1)}, u32[]{:S(2)}, u32[]{:S(2)}) %collective-permute-start) | collective-permute-done | bytes 557088 | tf_op jit(solution)/shard_map/cond/branch_0_fun/ppermute | solution.py:68
  (32 shorter events, 19.7 us)
Async XLA Ops:
  3.3 6.7 %copy-start = (bf16[4,128,2048]{2,1,0:T(8,128)(2,1)S(1)}, bf16[4,128,2048]{2,1,0:T(8,128)(2,1)}, u32[]{:S(2)}) copy-start(bf16[4,128,2048]{2,1,0:T(8,128)(2,1)} %shard_map.84.dep) | copy-start | bytes 6291460
  3.3 55.5 %all-to-all-start = ((bf16[4,128,2048]{2,1,0:T(8,128)(2,1)}), bf16[4,128,2048]{2,1,0:T(8,128)(2,1)}, u32[]{:S(2)}, u32[]{:S(2)}) async-start(bf16[4,128,2048]{2,1,0:T(8,128)(2,1)} %shard_map.84.dep), calls=%async_computation | async-start | bytes 4194304 | tf_op jit(solution)/shard_map/all_to_all | solution.py:72
  13.2 17.5 %collective-permute-start.6 = (bf16[192,1280]{1,0:T(8,128)(2,1)}, bf16[192,1280]{1,0:T(8,128)(2,1)S(1)}, u32[]{:S(2)}, u32[]{:S(2)}) collective-permute-start(bf16[192,1280]{1,0:T(8,128)(2,1)} %get-tuple-element.164.sa), channel_id=1, source_target_pairs={{0,1},{1,2},{2,3},{3,0},{4,5},{5,6},{6,7},{7,4},{8,9},{9,10},{10,1... | collective-permute-start | bytes 1474568 | tf_op jit(solution)/shard_map/ppermute | solution.py:68
  16.6 16.3 %collective-permute-start.7 = (bf16[192,1280]{1,0:T(8,128)(2,1)}, bf16[192,1280]{1,0:T(8,128)(2,1)S(1)}, u32[]{:S(2)}, u32[]{:S(2)}) collective-permute-start(bf16[192,1280]{1,0:T(8,128)(2,1)} %get-tuple-element.165.sb), channel_id=1, source_target_pairs={{0,3},{1,0},{2,1},{3,2},{4,7},{5,4},{6,5},{7,6},{8,11},{9,8},{10,9... | collective-permute-start | bytes 1474568 | tf_op jit(solution)/shard_map/ppermute | solution.py:68
  20.2 23.0 %collective-permute-start.4 = (bf16[192,1536]{1,0:T(8,128)(2,1)S(1)}, bf16[192,1536]{1,0:T(8,128)(2,1)S(1)}, u32[]{:S(2)}, u32[]{:S(2)}) collective-permute-start(bf16[192,1536]{1,0:T(8,128)(2,1)S(1)} %get-tuple-element.162), channel_id=1, source_target_pairs={{0,1},{1,2},{2,3},{3,0},{4,5},{5,6},{6,7},{7,4},{8,9},{9,10},{10,1... | collective-permute-start | bytes 1769480 | tf_op jit(solution)/shard_map/ppermute | solution.py:68
  22.4 23.0 %collective-permute-start.5 = (bf16[192,1536]{1,0:T(8,128)(2,1)S(1)}, bf16[192,1536]{1,0:T(8,128)(2,1)S(1)}, u32[]{:S(2)}, u32[]{:S(2)}) collective-permute-start(bf16[192,1536]{1,0:T(8,128)(2,1)S(1)} %get-tuple-element.163), channel_id=1, source_target_pairs={{0,3},{1,0},{2,1},{3,2},{4,7},{5,4},{6,5},{7,6},{8,11},{9,8},{10,9... | collective-permute-start | bytes 1769480 | tf_op jit(solution)/shard_map/ppermute | solution.py:68
  30.6 14.8 %copy-start.5 = (bf16[192,1280]{1,0:T(8,128)(2,1)}, bf16[192,1280]{1,0:T(8,128)(2,1)S(1)}, u32[]{:S(2)}) copy-start(bf16[192,1280]{1,0:T(8,128)(2,1)S(1)} %collective-permute-done.6.la) | copy-start | bytes 1474564
  30.6 21.4 %collective-permute-start.8 = (bf16[192,1280]{1,0:T(8,128)(2,1)S(1)}, bf16[192,1280]{1,0:T(8,128)(2,1)S(1)}, u32[]{:S(2)}, u32[]{:S(2)}) collective-permute-start(bf16[192,1280]{1,0:T(8,128)(2,1)S(1)} %collective-permute-done.6.la), channel_id=1, source_target_pairs={{0,1},{1,2},{2,3},{3,0},{4,5},{5,6},{6,7},{7,4},{8,9},{9,10},{10,1... | collective-permute-start | bytes 1474568 | tf_op jit(solution)/shard_map/ppermute | solution.py:68
  32.8 12.6 %copy-start.6 = (bf16[192,1280]{1,0:T(8,128)(2,1)}, bf16[192,1280]{1,0:T(8,128)(2,1)S(1)}, u32[]{:S(2)}) copy-start(bf16[192,1280]{1,0:T(8,128)(2,1)S(1)} %collective-permute-done.7.rb) | copy-start | bytes 1474564
  32.8 21.1 %collective-permute-start.9 = (bf16[192,1280]{1,0:T(8,128)(2,1)S(1)}, bf16[192,1280]{1,0:T(8,128)(2,1)S(1)}, u32[]{:S(2)}, u32[]{:S(2)}) collective-permute-start(bf16[192,1280]{1,0:T(8,128)(2,1)S(1)} %collective-permute-done.7.rb), channel_id=1, source_target_pairs={{0,3},{1,0},{2,1},{3,2},{4,7},{5,4},{6,5},{7,6},{8,11},{9,8},{10,9... | collective-permute-start | bytes 1474568 | tf_op jit(solution)/shard_map/ppermute | solution.py:68
  43.3 2.2 %copy-start.3 = (bf16[192,1536]{1,0:T(8,128)(2,1)}, bf16[192,1536]{1,0:T(8,128)(2,1)S(1)}, u32[]{:S(2)}) copy-start(bf16[192,1536]{1,0:T(8,128)(2,1)S(1)} %collective-permute-done.4.lt) | copy-start | bytes 1769476
  45.5 0.8 copy-start.4
  58.8 52.8 %all-to-all-start.1 = ((bf16[4,128,2048]{2,1,0:T(8,128)(2,1)}), bf16[4,128,2048]{2,1,0:T(8,128)(2,1)S(1)}, u32[]{:S(2)}, u32[]{:S(2)}) async-start(bf16[4,128,2048]{2,1,0:T(8,128)(2,1)} %shard_map.87.dep), calls=%async_computation.1 | async-start | bytes 4194304 | tf_op jit(solution)/shard_map/all_to_all | solution.py:72
  67.1 20.4 %collective-permute-start.11 = (bf16[192,1280]{1,0:T(8,128)(2,1)S(1)}, bf16[192,1280]{1,0:T(8,128)(2,1)S(1)}, u32[]{:S(2)}, u32[]{:S(2)}) collective-permute-start(bf16[192,1280]{1,0:T(8,128)(2,1)S(1)} %get-tuple-element.166.dep), channel_id=1, source_target_pairs={{0,1},{1,2},{2,3},{3,0},{4,5},{5,6},{6,7},{7,4},{8,9},{9,10},{10,1... | collective-permute-start | bytes 1474568 | tf_op jit(solution)/shard_map/ppermute | solution.py:68
  70.5 17.0 %collective-permute-start.12 = (bf16[192,1280]{1,0:T(8,128)(2,1)S(1)}, bf16[192,1280]{1,0:T(8,128)(2,1)S(1)}, u32[]{:S(2)}, u32[]{:S(2)}) collective-permute-start(bf16[192,1280]{1,0:T(8,128)(2,1)S(1)} %get-tuple-element.172), channel_id=1, source_target_pairs={{0,3},{1,0},{2,1},{3,2},{4,7},{5,4},{6,5},{7,6},{8,11},{9,8},{10,9... | collective-permute-start | bytes 1474568 | tf_op jit(solution)/shard_map/ppermute | solution.py:68
  80.3 31.3 %copy-start.1 = (bf16[128,2048]{1,0:T(8,128)(2,1)S(1)}, bf16[128,2048]{1,0:T(8,128)(2,1)}, u32[]{:S(2)}) copy-start(bf16[128,2048]{1,0:T(8,128)(2,1)} %weight_ref.3) | copy-start | bytes 1572868
  80.3 31.3 %copy-start.2 = (bf16[128]{0:T(256)(128)(2,1)S(1)}, bf16[128]{0:T(256)(128)(2,1)}, u32[]{:S(2)}) copy-start(bf16[128]{0:T(256)(128)(2,1)} %param.11) | copy-start | bytes 772
  80.3 32.0 %collective-permute-start.10 = (bf16[192,1536]{1,0:T(8,128)(2,1)}, bf16[192,1536]{1,0:T(8,128)(2,1)}, u32[]{:S(2)}, u32[]{:S(2)}) collective-permute-start(bf16[192,1536]{1,0:T(8,128)(2,1)} %get-tuple-element.169), channel_id=1, source_target_pairs={{0,1},{1,2},{2,3},{3,0},{4,5},{5,6},{6,7},{7,4},{8,9},{9,10},{10,1... | collective-permute-start | bytes 1769480 | tf_op jit(solution)/shard_map/ppermute | solution.py:68
  82.6 29.6 %collective-permute-start.14 = (bf16[192,1536]{1,0:T(8,128)(2,1)S(1)}, bf16[192,1536]{1,0:T(8,128)(2,1)}, u32[]{:S(2)}, u32[]{:S(2)}) collective-permute-start(bf16[192,1536]{1,0:T(8,128)(2,1)S(1)} %get-tuple-element.174), channel_id=1, source_target_pairs={{0,3},{1,0},{2,1},{3,2},{4,7},{5,4},{6,5},{7,6},{8,11},{9,8},{10,9... | collective-permute-start | bytes 1769480 | tf_op jit(solution)/shard_map/ppermute | solution.py:68
  88.6 18.1 %collective-permute-start.13 = (bf16[192,1280]{1,0:T(8,128)(2,1)}, bf16[192,1280]{1,0:T(8,128)(2,1)}, u32[]{:S(2)}, u32[]{:S(2)}) collective-permute-start(bf16[192,1280]{1,0:T(8,128)(2,1)} %get-tuple-element.173), channel_id=1, source_target_pairs={{0,1},{1,2},{2,3},{3,0},{4,5},{5,6},{6,7},{7,4},{8,9},{9,10},{10,1... | collective-permute-start | bytes 1474568 | tf_op jit(solution)/shard_map/ppermute | solution.py:68
  90.5 17.2 %collective-permute-start.15 = (bf16[192,1280]{1,0:T(8,128)(2,1)}, bf16[192,1280]{1,0:T(8,128)(2,1)}, u32[]{:S(2)}, u32[]{:S(2)}) collective-permute-start(bf16[192,1280]{1,0:T(8,128)(2,1)} %get-tuple-element.175), channel_id=1, source_target_pairs={{0,3},{1,0},{2,1},{3,2},{4,7},{5,4},{6,5},{7,6},{8,11},{9,8},{10,9... | collective-permute-start | bytes 1474568 | tf_op jit(solution)/shard_map/ppermute | solution.py:68
  112.3 18.5 %collective-permute-start = (bf16[128,2176]{1,0:T(8,128)(2,1)S(1)}, bf16[128,2176]{1,0:T(8,128)(2,1)S(1)}, u32[]{:S(2)}, u32[]{:S(2)}) collective-permute-start(bf16[128,2176]{1,0:T(8,128)(2,1)S(1)} %get-tuple-element.91.mine), channel_id=1, source_target_pairs={{0,16},{16,32},{32,48},{48,64},{64,80},{80,96},{96,112},{112,128},... | collective-permute-start | bytes 1671176 | tf_op jit(solution)/shard_map/cond/branch_0_fun/ppermute | solution.py:68

commit v4 on v3

--- a/solution.py
+++ b/solution.py
@@ -93,14 +93,12 @@
 
 
 def token_kernel(
-    n_x, me_ref, tok, up, dep, own_ref, sa_ref, sb_ref, ta_ref, tb_ref, rstd_ref, vt, vu, sems
+    n_x, me_ref, vt, vu, dep, own_ref, sa_ref, sb_ref, ta_ref, tb_ref, rstd_ref
 ):
-    fetched = fetch([(tok, vt), (up, vu)], sems)
     me = me_ref[0]
     width, part = vt.shape[1], own_ref.shape[1]
     rows = part // (width // part)
     half, quarter = width // 2, part // 2
-    fetched[0].wait()
     for d in range(n_x):
         slot = lax.rem(me + d, n_x) * rows
         for k in range(part // rows):
@@ -119,7 +117,6 @@
     x = vt[...].astype(F32)
     rstd = lax.rsqrt(jnp.mean(x * x, axis=1, keepdims=True) + eps)
     rstd_ref[...] = jnp.broadcast_to(rstd, rstd_ref.shape)
-    fetched[1].wait()
     up_a = (vu[:, :half].astype(F32) * rstd).astype(BF16)
     up_b = (vu[:, half:].astype(F32) * rstd).astype(BF16)
     sa_ref[:, :half] = up_a
@@ -283,22 +280,18 @@
     out_x[...] = (g - xhat * mean).astype(BF16)
 
 
-def step_kernel(parts_ref, weight_ref, gain_ref, dep_1, dep_2, out_ref):
-    width = weight_ref.shape[1]
-    column = column_of(gain_ref[...].astype(F32))
+def step_kernel(parts_ref, weight_ref, gain_ref, dep_1, dep_2, out_w_ref, out_g_ref):
+    gain = gain_ref[...].astype(F32)
     grad = jnp.sum(parts_ref[...].astype(F32), axis=0)
     w = weight_ref[...].astype(F32)
     slope = jnp.sum(grad * w, axis=1, keepdims=True)
-    out_ref[:, :width] = (w - step_rate * (column * grad)).astype(BF16)
-    stepped = (column - gain_rate * slope).astype(BF16)
-    out_ref[:, width:] = jnp.broadcast_to(stepped, (stepped.shape[0], out_ref.shape[1] - width))
-
-
-def mean_kernel(mine, peer, out_w_ref, out_g_ref):
-    width = out_w_ref.shape[1]
-    out_w_ref[...] = (0.5 * (mine[:, :width].astype(F32) + peer[:, :width].astype(F32))).astype(BF16)
-    column = 0.5 * (mine[:, width : width + 1].astype(F32) + peer[:, width : width + 1].astype(F32))
-    out_g_ref[...] = row_of(column).astype(BF16)
+    out_w_ref[...] = (w - step_rate * (column_of(gain) * grad)).astype(BF16)
+    out_g_ref[...] = (gain - gain_rate * row_of(slope)).astype(BF16)
+
+
+def mean_kernel(w_ref, pw_ref, g_ref, pg_ref, out_w_ref, out_g_ref):
+    out_w_ref[...] = (0.5 * (w_ref[...].astype(F32) + pw_ref[...].astype(F32))).astype(BF16)
+    out_g_ref[...] = (0.5 * (g_ref[...].astype(F32) + pg_ref[...].astype(F32))).astype(BF16)
 
 
 def on_device(tokens, weight, gain, upstream, step):
@@ -324,7 +317,7 @@
 
     x_own, sa, sb, ta, tb, rstd = call(
         functools.partial(token_kernel, n_x),
-        [(me, SCALAR), (tokens, ANY), (upstream, ANY), (copies, DEP)],
+        [(me, SCALAR), (tokens, HERE), (upstream, HERE), (copies, DEP)],
         [
             in_hbm((count, part)),
             in_hbm(short),
@@ -333,7 +326,6 @@
             array(long),
             in_hbm((count, 128), F32),
         ],
-        [vmem(count, width_in), vmem(count, width_out), sems(2)],
     )
     la, rb = shifted(sa, "x", 1), shifted(sb, "x", -1)
     lt, rt = shifted(ta, "x", 1), shifted(tb, "x", -1)
@@ -386,16 +378,16 @@
     )
     got_ld, got_rd = shifted(dr, "x", 1), shifted(dl, "x", -1)
 
-    (stepped,) = call(
+    stepped = call(
         step_kernel,
         [(v, HERE) for v in (pieces_w, weight, gain_row)] + [(got_ld, DEP), (got_rd, DEP)],
-        [array((rows, width_out + 128))],
+        [array((rows, width_out)), array((1, rows))],
         moved=moved,
     )
 
     def gossip(distance):
         def branch(stepped, rest):
-            peer = shifted(stepped, "rep", distance)
+            peer = [shifted(v, "rep", distance) for v in stepped]
             results = call(
                 functools.partial(result_kernel, n_x),
                 [(rest[0], SCALAR)] + [(v, BLOCK) for v in rest[1:]],
@@ -405,7 +397,7 @@
             )
             means = call(
                 mean_kernel,
-                [(stepped, HERE), (peer, HERE)],
+                [(v, HERE) for v in (stepped[0], peer[0], stepped[1], peer[1])],
                 [in_hbm((rows, width_out)), in_hbm((1, rows))],
             )
             return *results, *means

time: 133 us -> 149 us (1.12)
  the two profiles are of different devices: /device:TPU:24 before, /device:TPU:28 now
where the time goes in v4:
time: 149 us
  starting transfers between devices  59.6 us (40%)
  waiting for transfers between devices  57.6 us (39%)
  Pallas kernels  29.1 us (20%)
  between operations  1.49 us (1%)
    ppermute x14, waiting for transfers between devices, shifted(): return lax.ppermute(value, axis, pairs)  50.8 us
    ppermute x14, starting transfers between devices, shifted(): return lax.ppermute(value, axis, pairs)  48 us
    pallas_call x10, Pallas kernels, call(): pl.pallas_call(kernel, grid=(1,), out_shape=list(outs), in_specs=[whole(v...  29.1 us
    all_to_all x2, starting transfers between devices, exchange(): return lax.all_to_all(blocks, axis, split_axis=0, concat_axis=0, tiled=True)  11.6 us
    all_to_all x2, waiting for transfers between devices, exchange(): return lax.all_to_all(blocks, axis, split_axis=0, concat_axis=0, tiled=True)  6.72 us
  transfers between devices with their start and end apart: 16, of which 10 were waited for; matrix products, arithmetic and copies ran while one was open for 0% of the time, Pallas kernels for 17%

profile of v4, /device:TPU:28, one launch (start us, length us, event | category | flops | bytes accessed | tf_op | source)
XLA Modules:
  0.0 148.6 jit_solution(10982942444797240989)
XLA Ops:
  3.3 6.8 %all-to-all-start = ((bf16[4,128,2048]{2,1,0:T(8,128)(2,1)}), bf16[4,128,2048]{2,1,0:T(8,128)(2,1)}, u32[]{:S(2)}, u32[]{:S(2)}) async-start(bf16[4,128,2048]{2,1,0:T(8,128)(2,1)} %shard_map.84.dep), calls=%async_computation | async-start | bytes 4194304 | tf_op jit(solution)/shard_map/all_to_all | solution.py:72
  12.7 3.1 %collective-permute-start.10 = (bf16[192,1280]{1,0:T(8,128)(2,1)}, bf16[192,1280]{1,0:T(8,128)(2,1)S(1)}, u32[]{:S(2)}, u32[]{:S(2)}) collective-permute-start(bf16[192,1280]{1,0:T(8,128)(2,1)} %get-tuple-element.178.sa), channel_id=1, source_target_pairs={{0,1},{1,2},{2,3},{3,0},{4,5},{5,6},{6,7},{7,4},{8,9},{9,10},{10,1... | collective-permute-start | bytes 1474568 | tf_op jit(solution)/shard_map/ppermute | solution.py:68
  18.6 3.1 %collective-permute-start.8 = (bf16[192,1536]{1,0:T(8,128)(2,1)S(1)}, bf16[192,1536]{1,0:T(8,128)(2,1)S(1)}, u32[]{:S(2)}, u32[]{:S(2)}) collective-permute-start(bf16[192,1536]{1,0:T(8,128)(2,1)S(1)} %get-tuple-element.176), channel_id=1, source_target_pairs={{0,1},{1,2},{2,3},{3,0},{4,5},{5,6},{6,7},{7,4},{8,9},{9,10},{10,1... | collective-permute-start | bytes 1769480 | tf_op jit(solution)/shard_map/ppermute | solution.py:68
  21.7 2.7 %collective-permute-start.9 = (bf16[192,1536]{1,0:T(8,128)(2,1)S(1)}, bf16[192,1536]{1,0:T(8,128)(2,1)S(1)}, u32[]{:S(2)}, u32[]{:S(2)}) collective-permute-start(bf16[192,1536]{1,0:T(8,128)(2,1)S(1)} %get-tuple-element.177), channel_id=1, source_target_pairs={{0,3},{1,0},{2,1},{3,2},{4,7},{5,4},{6,5},{7,6},{8,11},{9,8},{10,9... | collective-permute-start | bytes 1769480 | tf_op jit(solution)/shard_map/ppermute | solution.py:68
  24.4 4.5 %collective-permute-done.10.la = bf16[192,1280]{1,0:T(8,128)(2,1)S(1)} collective-permute-done((bf16[192,1280]{1,0:T(8,128)(2,1)}, bf16[192,1280]{1,0:T(8,128)(2,1)S(1)}, u32[]{:S(2)}, u32[]{:S(2)}) %collective-permute-start.10) | collective-permute-done | bytes 491552 | tf_op jit(solution)/shard_map/ppermute | solution.py:68
  29.0 3.1 %collective-permute-start.12 = (bf16[192,1280]{1,0:T(8,128)(2,1)S(1)}, bf16[192,1280]{1,0:T(8,128)(2,1)S(1)}, u32[]{:S(2)}, u32[]{:S(2)}) collective-permute-start(bf16[192,1280]{1,0:T(8,128)(2,1)S(1)} %collective-permute-done.10.la), channel_id=1, source_target_pairs={{0,1},{1,2},{2,3},{3,0},{4,5},{5,6},{6,7},{7,4},{8,9},{9,10},{10,1... | collective-permute-start | bytes 1474568 | tf_op jit(solution)/shard_map/ppermute | solution.py:68
  32.1 2.7 %collective-permute-start.13 = (bf16[192,1280]{1,0:T(8,128)(2,1)S(1)}, bf16[192,1280]{1,0:T(8,128)(2,1)S(1)}, u32[]{:S(2)}, u32[]{:S(2)}) collective-permute-start(bf16[192,1280]{1,0:T(8,128)(2,1)S(1)} %collective-permute-done.11.rb), channel_id=1, source_target_pairs={{0,3},{1,0},{2,1},{3,2},{4,7},{5,4},{6,5},{7,6},{8,11},{9,8},{10,9... | collective-permute-start | bytes 1474568 | tf_op jit(solution)/shard_map/ppermute | solution.py:68
  34.9 6.8 %collective-permute-done.8.lt = bf16[192,1536]{1,0:T(8,128)(2,1)S(1)} collective-permute-done((bf16[192,1536]{1,0:T(8,128)(2,1)S(1)}, bf16[192,1536]{1,0:T(8,128)(2,1)S(1)}, u32[]{:S(2)}, u32[]{:S(2)}) %collective-permute-start.8) | collective-permute-done | bytes 589856 | tf_op jit(solution)/shard_map/ppermute | solution.py:68
  41.6 3.1 %collective-permute-done.9.rt = bf16[192,1536]{1,0:T(8,128)(2,1)S(1)} collective-permute-done((bf16[192,1536]{1,0:T(8,128)(2,1)S(1)}, bf16[192,1536]{1,0:T(8,128)(2,1)S(1)}, u32[]{:S(2)}, u32[]{:S(2)}) %collective-permute-start.9) | collective-permute-done | bytes 589856 | tf_op jit(solution)/shard_map/ppermute | solution.py:68
  45.6 4.6 %shard_map.86.near = f32[512,2048]{1,0:T(8,128)S(1)} custom-call(bf16[192,512]{1,0:T(8,128)(2,1)} %get-tuple-element.175.xo, bf16[192,1536]{1,0:T(8,128)(2,1)} %copy-done.4, bf16[192,1536]{1,0:T(8,128)(2,1)} %copy-done.5, bf16[192,1280]{1,0:T(8,128)(2,1)} %get-tuple-element.178.sa, bf16[192,1280]{1,0:T(8,128)(2,1)} %copy-done.6, ...), custom_call_target="tpu_custom_call" | custom-call | flops 1207959552 | bytes 6029312 | tf_op jit(solution)/shard_map/pallas_call | solution.py:38
  50.4 2.8 %collective-permute-done.13.fb = bf16[192,1280]{1,0:T(8,128)(2,1)S(1)} collective-permute-done((bf16[192,1280]{1,0:T(8,128)(2,1)S(1)}, bf16[192,1280]{1,0:T(8,128)(2,1)S(1)}, u32[]{:S(2)}, u32[]{:S(2)}) %collective-permute-start.13) | collective-permute-done | bytes 491552 | tf_op jit(solution)/shard_map/ppermute | solution.py:68
  53.2 3.2 %shard_map.87.dep = bf16[4,128,2048]{2,1,0:T(8,128)(2,1)} custom-call(f32[512,2048]{1,0:T(8,128)S(1)} %shard_map.86.near, bf16[192,1280]{1,0:T(8,128)(2,1)S(1)} %collective-permute-done.12.fa, bf16[192,1280]{1,0:T(8,128)(2,1)S(1)} %collective-permute-done.13.fb), custom_call_target="tpu_custom_call" | custom-call | flops 402653184 | bytes 6029312 | tf_op jit(solution)/shard_map/pallas_call | solution.py:38
  58.9 4.8 %all-to-all-start.1 = ((bf16[4,128,2048]{2,1,0:T(8,128)(2,1)}), bf16[4,128,2048]{2,1,0:T(8,128)(2,1)S(1)}, u32[]{:S(2)}, u32[]{:S(2)}) async-start(bf16[4,128,2048]{2,1,0:T(8,128)(2,1)} %shard_map.87.dep), calls=%async_computation.1 | async-start | bytes 4194304 | tf_op jit(solution)/shard_map/all_to_all | solution.py:72
  66.4 3.6 %collective-permute-start.15 = (bf16[192,1280]{1,0:T(8,128)(2,1)S(1)}, bf16[192,1280]{1,0:T(8,128)(2,1)S(1)}, u32[]{:S(2)}, u32[]{:S(2)}) collective-permute-start(bf16[192,1280]{1,0:T(8,128)(2,1)S(1)} %get-tuple-element.180.dep), channel_id=1, source_target_pairs={{0,1},{1,2},{2,3},{3,0},{4,5},{5,6},{6,7},{7,4},{8,9},{9,10},{10,1... | collective-permute-start | bytes 1474568 | tf_op jit(solution)/shard_map/ppermute | solution.py:68
  72.3 6.1 %shard_map.89 = (f32[192,2048]{1,0:T(8,128)}, bf16[192,512]{1,0:T(8,128)(2,1)}, bf16[192,1536]{1,0:T(8,128)(2,1)}, bf16[192,1536]{1,0:T(8,128)(2,1)S(1)}, f32[19...) custom-call(bf16[192,512]{1,0:T(8,128)(2,1)} %get-tuple-element.175.xo, bf16[192,1536]{1,0:T(8,128)(2,1)} %copy-done.4, ...), custom_call_target="tpu_custom_call" | custom-call | flops 3221225472 | bytes 12058624 | tf_op jit(solution)/shard_map/pallas_call | solution.py:38
  78.4 3.7 %collective-permute-start.14 = (bf16[192,1536]{1,0:T(8,128)(2,1)}, bf16[192,1536]{1,0:T(8,128)(2,1)}, u32[]{:S(2)}, u32[]{:S(2)}) collective-permute-start(bf16[192,1536]{1,0:T(8,128)(2,1)} %get-tuple-element.183), channel_id=1, source_target_pairs={{0,1},{1,2},{2,3},{3,0},{4,5},{5,6},{6,7},{7,4},{8,9},{9,10},{10,1... | collective-permute-start | bytes 1769480 | tf_op jit(solution)/shard_map/ppermute | solution.py:68
  85.4 3.6 %collective-permute-start.17 = (bf16[192,1280]{1,0:T(8,128)(2,1)}, bf16[192,1280]{1,0:T(8,128)(2,1)}, u32[]{:S(2)}, u32[]{:S(2)}) collective-permute-start(bf16[192,1280]{1,0:T(8,128)(2,1)} %get-tuple-element.187), channel_id=1, source_target_pairs={{0,1},{1,2},{2,3},{3,0},{4,5},{5,6},{6,7},{7,4},{8,9},{9,10},{10,1... | collective-permute-start | bytes 1474568 | tf_op jit(solution)/shard_map/ppermute | solution.py:68
  91.9 11.6 %collective-permute-done.17.dep_1 = bf16[192,1280]{1,0:T(8,128)(2,1)} collective-permute-done((bf16[192,1280]{1,0:T(8,128)(2,1)}, bf16[192,1280]{1,0:T(8,128)(2,1)}, u32[]{:S(2)}, u32[]{:S(2)}) %collective-permute-start.17) | collective-permute-done | bytes 491552 | tf_op jit(solution)/shard_map/ppermute | solution.py:68
  103.5 3.1 %collective-permute-done.19.dep_2 = bf16[192,1280]{1,0:T(8,128)(2,1)} collective-permute-done((bf16[192,1280]{1,0:T(8,128)(2,1)}, bf16[192,1280]{1,0:T(8,128)(2,1)}, u32[]{:S(2)}, u32[]{:S(2)}) %collective-permute-start.19) | collective-permute-done | bytes 491552 | tf_op jit(solution)/shard_map/ppermute | solution.py:68
  106.6 4.3 %all-to-all-done.1.parts_ref = bf16[4,128,2048]{2,1,0:T(8,128)(2,1)S(1)} async-done(((bf16[4,128,2048]{2,1,0:T(8,128)(2,1)}), bf16[4,128,2048]{2,1,0:T(8,128)(2,1)S(1)}, u32[]{:S(2)}, u32[]{:S(2)}) %all-to-all-start.1) | async-done | bytes 2097184 | tf_op jit(solution)/shard_map/all_to_all | solution.py:72
  111.6 37.1 %conditional.1 = (bf16[192,2048]{1,0:T(8,128)(2,1)}, bf16[192,2048]{1,0:T(8,128)(2,1)}, bf16[128,2048]{1,0:T(8,128)(2,1)}, bf16[1,128]{1,0:T(2,128)(2,1)}) conditional(s32[]{:T(128)} %clamp.3, (s32[2]{0:T(128)S(1)}, bf16[192,2048]{1,0:T(8,128)(2,1)}, f32[192,128]{1,0:T(8,128)}, f32[192,2048]{1,0:T(8,128)}, ...), branch_computations={%region_0.1_spmd, %region_1.2_spmd, %region_2.3_spmd, %region_3.4_... | conditional | bytes 8127600 | solution.py:407
  111.6 10.9 %collective-permute-start.6 = (bf16[128,2048]{1,0:T(8,128)(2,1)S(1)}, bf16[128,2048]{1,0:T(8,128)(2,1)S(1)}, u32[]{:S(2)}, u32[]{:S(2)}) collective-permute-start(bf16[128,2048]{1,0:T(8,128)(2,1)S(1)} %get-tuple-element.144.w_ref), channel_id=1, source_target_pairs={{0,128},{16,144},{32,160},{48,176},{64,192},{80,208},{96,224},{112... | collective-permute-start | bytes 1572872 | tf_op jit(solution)/shard_map/cond/branch_3_fun/ppermute | solution.py:68
  124.5 4.5 %branch_3_fun.2 = (bf16[192,2048]{1,0:T(8,128)(2,1)}, bf16[192,2048]{1,0:T(8,128)(2,1)}) custom-call(s32[2]{0:T(128)S(1)} %get-tuple-element.133.me_ref, bf16[192,2048]{1,0:T(8,128)(2,1)} %get-tuple-element.134.tok_ref, f32[192,128]{1,0:T(8,128)} %get-tuple-element.135.rstd_ref, f32[192,2048]{1,0:T(8,128)} %get-tuple-element.136.p0, ...), custom_call_target="tpu_custom_call" | custom-call | bytes 6029312 | tf_op jit(solution)/shard_map/cond/branch_3_fun/pallas_call | solution.py:38
  129.0 18.7 %collective-permute-done.7.pg_ref = bf16[1,128]{1,0:T(2,128)(2,1)S(1)} collective-permute-done((bf16[1,128]{1,0:T(2,128)(2,1)S(1)}, bf16[1,128]{1,0:T(2,128)(2,1)S(1)}, u32[]{:S(2)}, u32[]{:S(2)}) %collective-permute-start.7) | collective-permute-done | bytes 288 | tf_op jit(solution)/shard_map/cond/branch_3_fun/ppermute | solution.py:68
  (36 shorter events, 25.6 us)
Async XLA Ops:
  3.3 6.9 %copy-start = (bf16[4,128,2048]{2,1,0:T(8,128)(2,1)S(1)}, bf16[4,128,2048]{2,1,0:T(8,128)(2,1)}, u32[]{:S(2)}) copy-start(bf16[4,128,2048]{2,1,0:T(8,128)(2,1)} %shard_map.84.dep) | copy-start | bytes 6291460
  3.3 6.9 %copy-start.2 = (bf16[192,2048]{1,0:T(8,128)(2,1)S(1)}, bf16[192,2048]{1,0:T(8,128)(2,1)}, u32[]{:S(2)}) copy-start(bf16[192,2048]{1,0:T(8,128)(2,1)} %vu.1) | copy-start | bytes 2359300
  3.3 55.6 %all-to-all-start = ((bf16[4,128,2048]{2,1,0:T(8,128)(2,1)}), bf16[4,128,2048]{2,1,0:T(8,128)(2,1)}, u32[]{:S(2)}, u32[]{:S(2)}) async-start(bf16[4,128,2048]{2,1,0:T(8,128)(2,1)} %shard_map.84.dep), calls=%async_computation | async-start | bytes 4194304 | tf_op jit(solution)/shard_map/all_to_all | solution.py:72
  12.7 16.3 %collective-permute-start.10 = (bf16[192,1280]{1,0:T(8,128)(2,1)}, bf16[192,1280]{1,0:T(8,128)(2,1)S(1)}, u32[]{:S(2)}, u32[]{:S(2)}) collective-permute-start(bf16[192,1280]{1,0:T(8,128)(2,1)} %get-tuple-element.178.sa), channel_id=1, source_target_pairs={{0,1},{1,2},{2,3},{3,0},{4,5},{5,6},{6,7},{7,4},{8,9},{9,10},{10,1... | collective-permute-start | bytes 1474568 | tf_op jit(solution)/shard_map/ppermute | solution.py:68
  15.8 16.3 %collective-permute-start.11 = (bf16[192,1280]{1,0:T(8,128)(2,1)}, bf16[192,1280]{1,0:T(8,128)(2,1)S(1)}, u32[]{:S(2)}, u32[]{:S(2)}) collective-permute-start(bf16[192,1280]{1,0:T(8,128)(2,1)} %get-tuple-element.179.sb), channel_id=1, source_target_pairs={{0,3},{1,0},{2,1},{3,2},{4,7},{5,4},{6,5},{7,6},{8,11},{9,8},{10,9... | collective-permute-start | bytes 1474568 | tf_op jit(solution)/shard_map/ppermute | solution.py:68
  18.6 23.0 %collective-permute-start.8 = (bf16[192,1536]{1,0:T(8,128)(2,1)S(1)}, bf16[192,1536]{1,0:T(8,128)(2,1)S(1)}, u32[]{:S(2)}, u32[]{:S(2)}) collective-permute-start(bf16[192,1536]{1,0:T(8,128)(2,1)S(1)} %get-tuple-element.176), channel_id=1, source_target_pairs={{0,1},{1,2},{2,3},{3,0},{4,5},{5,6},{6,7},{7,4},{8,9},{9,10},{10,1... | collective-permute-start | bytes 1769480 | tf_op jit(solution)/shard_map/ppermute | solution.py:68
  21.7 23.0 %collective-permute-start.9 = (bf16[192,1536]{1,0:T(8,128)(2,1)S(1)}, bf16[192,1536]{1,0:T(8,128)(2,1)S(1)}, u32[]{:S(2)}, u32[]{:S(2)}) collective-permute-start(bf16[192,1536]{1,0:T(8,128)(2,1)S(1)} %get-tuple-element.177), channel_id=1, source_target_pairs={{0,3},{1,0},{2,1},{3,2},{4,7},{5,4},{6,5},{7,6},{8,11},{9,8},{10,9... | collective-permute-start | bytes 1769480 | tf_op jit(solution)/shard_map/ppermute | solution.py:68
  29.0 15.8 %copy-start.6 = (bf16[192,1280]{1,0:T(8,128)(2,1)}, bf16[192,1280]{1,0:T(8,128)(2,1)S(1)}, u32[]{:S(2)}) copy-start(bf16[192,1280]{1,0:T(8,128)(2,1)S(1)} %collective-permute-done.10.la) | copy-start | bytes 1474564
  29.0 21.4 %collective-permute-start.12 = (bf16[192,1280]{1,0:T(8,128)(2,1)S(1)}, bf16[192,1280]{1,0:T(8,128)(2,1)S(1)}, u32[]{:S(2)}, u32[]{:S(2)}) collective-permute-start(bf16[192,1280]{1,0:T(8,128)(2,1)S(1)} %collective-permute-done.10.la), channel_id=1, source_target_pairs={{0,1},{1,2},{2,3},{3,0},{4,5},{5,6},{6,7},{7,4},{8,9},{9,10},{10,1... | collective-permute-start | bytes 1474568 | tf_op jit(solution)/shard_map/ppermute | solution.py:68
  32.1 12.6 %copy-start.7 = (bf16[192,1280]{1,0:T(8,128)(2,1)}, bf16[192,1280]{1,0:T(8,128)(2,1)S(1)}, u32[]{:S(2)}) copy-start(bf16[192,1280]{1,0:T(8,128)(2,1)S(1)} %collective-permute-done.11.rb) | copy-start | bytes 1474564
  32.1 21.1 %collective-permute-start.13 = (bf16[192,1280]{1,0:T(8,128)(2,1)S(1)}, bf16[192,1280]{1,0:T(8,128)(2,1)S(1)}, u32[]{:S(2)}, u32[]{:S(2)}) collective-permute-start(bf16[192,1280]{1,0:T(8,128)(2,1)S(1)} %collective-permute-done.11.rb), channel_id=1, source_target_pairs={{0,3},{1,0},{2,1},{3,2},{4,7},{5,4},{6,5},{7,6},{8,11},{9,8},{10,9... | collective-permute-start | bytes 1474568 | tf_op jit(solution)/shard_map/ppermute | solution.py:68
  41.6 3.1 %copy-start.4 = (bf16[192,1536]{1,0:T(8,128)(2,1)}, bf16[192,1536]{1,0:T(8,128)(2,1)S(1)}, u32[]{:S(2)}) copy-start(bf16[192,1536]{1,0:T(8,128)(2,1)S(1)} %collective-permute-done.8.lt) | copy-start | bytes 1769476
  44.7 0.8 copy-start.5
  58.9 52.0 %all-to-all-start.1 = ((bf16[4,128,2048]{2,1,0:T(8,128)(2,1)}), bf16[4,128,2048]{2,1,0:T(8,128)(2,1)S(1)}, u32[]{:S(2)}, u32[]{:S(2)}) async-start(bf16[4,128,2048]{2,1,0:T(8,128)(2,1)} %shard_map.87.dep), calls=%async_computation.1 | async-start | bytes 4194304 | tf_op jit(solution)/shard_map/all_to_all | solution.py:72
  66.4 17.9 %collective-permute-start.15 = (bf16[192,1280]{1,0:T(8,128)(2,1)S(1)}, bf16[192,1280]{1,0:T(8,128)(2,1)S(1)}, u32[]{:S(2)}, u32[]{:S(2)}) collective-permute-start(bf16[192,1280]{1,0:T(8,128)(2,1)S(1)} %get-tuple-element.180.dep), channel_id=1, source_target_pairs={{0,1},{1,2},{2,3},{3,0},{4,5},{5,6},{6,7},{7,4},{8,9},{9,10},{10,1... | collective-permute-start | bytes 1474568 | tf_op jit(solution)/shard_map/ppermute | solution.py:68
  70.0 14.3 %collective-permute-start.16 = (bf16[192,1280]{1,0:T(8,128)(2,1)S(1)}, bf16[192,1280]{1,0:T(8,128)(2,1)S(1)}, u32[]{:S(2)}, u32[]{:S(2)}) collective-permute-start(bf16[192,1280]{1,0:T(8,128)(2,1)S(1)} %get-tuple-element.186), channel_id=1, source_target_pairs={{0,3},{1,0},{2,1},{3,2},{4,7},{5,4},{6,5},{7,6},{8,11},{9,8},{10,9... | collective-permute-start | bytes 1474568 | tf_op jit(solution)/shard_map/ppermute | solution.py:68
  78.3 32.6 %copy-start.1 = (bf16[128,2048]{1,0:T(8,128)(2,1)S(1)}, bf16[128,2048]{1,0:T(8,128)(2,1)}, u32[]{:S(2)}) copy-start(bf16[128,2048]{1,0:T(8,128)(2,1)} %weight_ref.3) | copy-start | bytes 1572868
  78.3 32.6 %copy-start.3 = (bf16[128]{0:T(256)(128)(2,1)S(1)}, bf16[128]{0:T(256)(128)(2,1)}, u32[]{:S(2)}) copy-start(bf16[128]{0:T(256)(128)(2,1)} %param.11) | copy-start | bytes 772
  78.4 33.2 %collective-permute-start.14 = (bf16[192,1536]{1,0:T(8,128)(2,1)}, bf16[192,1536]{1,0:T(8,128)(2,1)}, u32[]{:S(2)}, u32[]{:S(2)}) collective-permute-start(bf16[192,1536]{1,0:T(8,128)(2,1)} %get-tuple-element.183), channel_id=1, source_target_pairs={{0,1},{1,2},{2,3},{3,0},{4,5},{5,6},{6,7},{7,4},{8,9},{9,10},{10,1... | collective-permute-start | bytes 1769480 | tf_op jit(solution)/shard_map/ppermute | solution.py:68
  82.1 29.5 %collective-permute-start.18 = (bf16[192,1536]{1,0:T(8,128)(2,1)S(1)}, bf16[192,1536]{1,0:T(8,128)(2,1)}, u32[]{:S(2)}, u32[]{:S(2)}) collective-permute-start(bf16[192,1536]{1,0:T(8,128)(2,1)S(1)} %get-tuple-element.188), channel_id=1, source_target_pairs={{0,3},{1,0},{2,1},{3,2},{4,7},{5,4},{6,5},{7,6},{8,11},{9,8},{10,9... | collective-permute-start | bytes 1769480 | tf_op jit(solution)/shard_map/ppermute | solution.py:68
  85.4 18.1 %collective-permute-start.17 = (bf16[192,1280]{1,0:T(8,128)(2,1)}, bf16[192,1280]{1,0:T(8,128)(2,1)}, u32[]{:S(2)}, u32[]{:S(2)}) collective-permute-start(bf16[192,1280]{1,0:T(8,128)(2,1)} %get-tuple-element.187), channel_id=1, source_target_pairs={{0,1},{1,2},{2,3},{3,0},{4,5},{5,6},{6,7},{7,4},{8,9},{9,10},{10,1... | collective-permute-start | bytes 1474568 | tf_op jit(solution)/shard_map/ppermute | solution.py:68
  89.0 17.6 %collective-permute-start.19 = (bf16[192,1280]{1,0:T(8,128)(2,1)}, bf16[192,1280]{1,0:T(8,128)(2,1)}, u32[]{:S(2)}, u32[]{:S(2)}) collective-permute-start(bf16[192,1280]{1,0:T(8,128)(2,1)} %get-tuple-element.189), channel_id=1, source_target_pairs={{0,3},{1,0},{2,1},{3,2},{4,7},{5,4},{6,5},{7,6},{8,11},{9,8},{10,9... | collective-permute-start | bytes 1474568 | tf_op jit(solution)/shard_map/ppermute | solution.py:68
  111.6 36.1 %collective-permute-start.6 = (bf16[128,2048]{1,0:T(8,128)(2,1)S(1)}, bf16[128,2048]{1,0:T(8,128)(2,1)S(1)}, u32[]{:S(2)}, u32[]{:S(2)}) collective-permute-start(bf16[128,2048]{1,0:T(8,128)(2,1)S(1)} %get-tuple-element.144.w_ref), channel_id=1, source_target_pairs={{0,128},{16,144},{32,160},{48,176},{64,192},{80,208},{96,224},{112... | collective-permute-start | bytes 1572872 | tf_op jit(solution)/shard_map/cond/branch_3_fun/ppermute | solution.py:68
  122.6 25.1 %collective-permute-start.7 = (bf16[1,128]{1,0:T(2,128)(2,1)S(1)}, bf16[1,128]{1,0:T(2,128)(2,1)S(1)}, u32[]{:S(2)}, u32[]{:S(2)}) collective-permute-start(bf16[1,128]{1,0:T(2,128)(2,1)S(1)} %get-tuple-element.145.g_ref), channel_id=1, source_target_pairs={{0,128},{16,144},{32,160},{48,176},{64,192},{80,208},{96,224},{112... | collective-permute-start | bytes 776 | tf_op jit(solution)/shard_map/cond/branch_3_fun/ppermute | solution.py:68
